TPU v7x, 512 devices: a whole 4x8x8 slice. The times are simulated.
512 devices in a mesh: dp: 8 (over x, core), seq: 64 (over z, y).
Axes of the slice: x: 4, y: 8, z: 8, core: 2. Of those that a mesh axis runs over, the one named last changes fastest.
Arguments:
- inputs: bfloat16 [8, 16384, 960], P('dp', 'seq'), may hold values from -6 to 6
- cotangent: bfloat16 [8, 16384, 960], P('dp', 'seq'), may hold values from -6 to 6
- kernel: bfloat16 [16384, 960], P('seq'), may hold values from -6 to 6
- mix_in: bfloat16 [16384, 256], P('seq'), may hold values from -0.375 to 0.375
- mix_out: bfloat16 [16384, 256], P('seq'), may hold values from -0.375 to 0.375
- twiddle_self: bfloat16 [2, 6, 16384], P(None, None, 'seq'), may hold values from 0.796875 to 1.1953125
- twiddle_cross: bfloat16 [2, 6, 16384], P(None, None, 'seq'), may hold values from -0.59765625 to 0.59765625
- norm_gain: bfloat16 [960], replicated, may hold values from 0.5 to 1.5
- up_weight: bfloat16 [240, 1920], replicated, may hold values from -0.375 to 0.375
- down_weight: bfloat16 [240, 1920], replicated, may hold values from -0.25 to 0.25
Outputs:
- output: bfloat16 [8, 16384, 960], P('dp', 'seq')
- input_grad: bfloat16 [8, 16384, 960], P('dp', 'seq')
- kernel_grad: bfloat16 [16384, 960], P('seq')
- up_grad: float32 [240, 1920], P(None, 'seq')
- down_grad: float32 [240, 1920], P(None, 'seq')
- gain_grad: float32 [960], P('seq')
All inputs are finite; a program needn't handle non-finite values.
Results may differ from a plain program's by a relative error of at most 0.02.
Values may be sent and summed in bfloat16 or wider, within the bound.
A program may use at most 64 MiB of HBM per device.

v0:
```python
import jax
import jax.numpy as jnp
from jax import lax
from jax.sharding import PartitionSpec as P

BLOCKS = 4


root_half = 0.7978845608028654
cubic_term = 0.044715


def swapped(value, axis, apart):
    mask = 2**apart
    pairs = [(source, source ^ mask) for source in range(lax.axis_size(axis))]
    return lax.ppermute(value, axis, pairs)


def rounded(values):
    return lax.optimization_barrier(values.astype(jnp.bfloat16))


def gelu_value(preact):
    inner_arg = root_half * (preact + cubic_term * preact * preact * preact)
    return 0.5 * preact * (1.0 + jnp.tanh(inner_arg))


def gelu_slope(preact):
    inner_arg = root_half * (preact + cubic_term * preact * preact * preact)
    tangent = jnp.tanh(inner_arg)
    return 0.5 * (1.0 + tangent) + 0.5 * preact * (1.0 - tangent * tangent) * root_half * (
        1.0 + 3.0 * cubic_term * preact * preact
    )


def pair_sections(values, self_rows, cross_rows):
    for section_index in range(self_rows.shape[0]):
        partner = swapped(values, "seq", section_index)
        values = rounded(
            self_rows[section_index][:, None].astype(jnp.float32) * values.astype(jnp.float32)
            + cross_rows[section_index][:, None].astype(jnp.float32) * partner.astype(jnp.float32)
        )
    return values


def pair_sections_back(gradient, self_rows, cross_rows):
    for section_index in reversed(range(self_rows.shape[0])):
        partner, partner_cross = swapped(
            (gradient, cross_rows[section_index][:, None]), "seq", section_index
        )
        gradient = rounded(
            self_rows[section_index][:, None].astype(jnp.float32) * gradient.astype(jnp.float32)
            + partner_cross.astype(jnp.float32) * partner.astype(jnp.float32)
        )
    return gradient


def local(
    inputs,
    cotangent,
    kernel,
    mix_in,
    mix_out,
    twiddle_self,
    twiddle_cross,
    norm_gain,
    up_weight,
    down_weight,
):
    token_count = inputs.shape[1]
    model_width = inputs.shape[2]
    block_count = BLOCKS
    block_width = model_width // block_count
    hidden_width = up_weight.shape[1] // block_count
    seq_in = inputs[0]
    seq_cot = cotangent[0]
    premixed = rounded(jnp.dot(mix_in, seq_in, preferred_element_type=jnp.float32))
    spectrum = pair_sections(premixed, twiddle_self[0], twiddle_cross[0])
    weighted = rounded(spectrum.astype(jnp.float32) * kernel.astype(jnp.float32))
    mixed_seq = pair_sections(weighted, twiddle_self[1], twiddle_cross[1])
    hidden = rounded(
        seq_in.astype(jnp.float32) + jnp.dot(mix_out, mixed_seq, preferred_element_type=jnp.float32)
    )
    widened = hidden.astype(jnp.float32)
    gain_wide = norm_gain.astype(jnp.float32)
    row_scale = lax.rsqrt(jnp.mean(widened * widened, axis=-1, keepdims=True) + 1e-06)
    normed = rounded(widened * row_scale * gain_wide)
    normed_blocks = normed.reshape(token_count, block_count, block_width)
    up_blocks = up_weight.reshape(block_width, block_count, hidden_width)
    down_blocks = down_weight.reshape(block_width, block_count, hidden_width)
    pre_act = jnp.einsum(
        "tgd,dgf->tgf", normed_blocks, up_blocks, preferred_element_type=jnp.float32
    )
    activation = rounded(gelu_value(pre_act))
    channel_out = jnp.einsum(
        "tgf,jgf->tgj", activation, down_blocks, preferred_element_type=jnp.float32
    )
    output = (widened + channel_out.transpose(0, 2, 1).reshape(token_count, model_width)).astype(
        jnp.bfloat16
    )
    cot_blocks = seq_cot.reshape(token_count, block_width, block_count).transpose(0, 2, 1)
    down_term = jnp.einsum(
        "tgf,tgj->jgf", activation, cot_blocks, preferred_element_type=jnp.float32
    )
    act_cot = jnp.einsum(
        "tgj,jgf->tgf", cot_blocks, down_blocks, preferred_element_type=jnp.float32
    )
    pre_grad = rounded(act_cot * gelu_slope(pre_act))
    up_term = jnp.einsum(
        "tgf,tgd->dgf", pre_grad, normed_blocks, preferred_element_type=jnp.float32
    )
    normed_grad = jnp.einsum(
        "tgf,dgf->tgd", pre_grad, up_blocks, preferred_element_type=jnp.float32
    ).reshape(token_count, model_width)
    gain_term = jnp.sum(normed_grad * widened * row_scale, axis=0)
    gained = normed_grad * gain_wide
    hidden_grad = rounded(
        seq_cot.astype(jnp.float32)
        + row_scale * gained
        - widened * row_scale**3 * jnp.mean(gained * widened, axis=-1, keepdims=True)
    )
    mixed_grad = rounded(
        lax.dot_general(
            mix_out, hidden_grad, (((0,), (0,)), ((), ())), preferred_element_type=jnp.float32
        )
    )
    up_part, down_part, gain_part = (
        lax.psum_scatter(up_term.reshape(block_width, -1), "seq", scatter_dimension=1, tiled=True),
        lax.psum_scatter(
            down_term.reshape(block_width, -1), "seq", scatter_dimension=1, tiled=True
        ),
        lax.psum_scatter(gain_term[None, :], "seq", scatter_dimension=1, tiled=True),
    )
    up_sum, down_sum, gain_sum = lax.psum((up_part, down_part, gain_part), "dp")
    weighted_grad = pair_sections_back(mixed_grad, twiddle_self[1], twiddle_cross[1])
    kernel_grad = lax.psum(
        spectrum.astype(jnp.float32) * weighted_grad.astype(jnp.float32), "dp"
    ).astype(jnp.bfloat16)
    spectrum_grad = rounded(weighted_grad.astype(jnp.float32) * kernel.astype(jnp.float32))
    pre_cot = pair_sections_back(spectrum_grad, twiddle_self[0], twiddle_cross[0])
    input_grad = (
        hidden_grad.astype(jnp.float32)
        + lax.dot_general(
            mix_in, pre_cot, (((0,), (0,)), ((), ())), preferred_element_type=jnp.float32
        )
    ).astype(jnp.bfloat16)
    scale_factor = (lax.axis_size("dp") * lax.axis_size("seq") * token_count) ** (-0.5)
    return (
        output[None],
        input_grad[None],
        kernel_grad,
        up_sum * scale_factor,
        down_sum * scale_factor,
        gain_sum[0] * scale_factor,
    )


def solution(mesh):
    in_specs = (
        P("dp", "seq", None),
        P("dp", "seq", None),
        P("seq", None),
        P("seq", None),
        P("seq", None),
        P(None, None, "seq"),
        P(None, None, "seq"),
        P(),
        P(),
        P(),
    )
    out_specs = (
        P("dp", "seq", None),
        P("dp", "seq", None),
        P("seq", None),
        P(None, "seq"),
        P(None, "seq"),
        P("seq"),
    )
    return jax.shard_map(local, mesh=mesh, in_specs=in_specs, out_specs=out_specs, check_vma=False)
```

profile of v0, /device:TPU:1, one launch (start us, length us, event | category | flops | bytes accessed | tf_op | source)
XLA Modules:
  0.0 916.3 jit_solution(8938115127478244982)
XLA Ops:
  2.1 4.0 collective-permute-start
  7.7 4.6 collective-permute-done
  12.5 8.8 collective-permute-start.1
  21.3 21.1 %collective-permute-done.1 = bf16[256,960]{0,1:T(8,128)(2,1)S(1)} collective-permute-done((bf16[256,960]{0,1:T(8,128)(2,1)S(1)}, bf16[256,960]{0,1:T(8,128)(2,1)S(1)}, u32[]{:S(2)}, u32[]{:S(2)}) %collective-permute-start.1) | collective-permute-done | bytes 491552 | tf_op jit(solution)/shard_map/ppermute | solution.py:16
  42.6 8.5 collective-permute-start.2
  51.1 21.6 %collective-permute-done.2 = bf16[256,960]{0,1:T(8,128)(2,1)S(1)} collective-permute-done((bf16[256,960]{0,1:T(8,128)(2,1)S(1)}, bf16[256,960]{0,1:T(8,128)(2,1)S(1)}, u32[]{:S(2)}, u32[]{:S(2)}) %collective-permute-start.2) | collective-permute-done | bytes 491552 | tf_op jit(solution)/shard_map/ppermute | solution.py:16
  72.9 3.9 collective-permute-start.3
  76.9 10.2 %collective-permute-done.3 = bf16[256,960]{0,1:T(8,128)(2,1)S(1)} collective-permute-done((bf16[256,960]{0,1:T(8,128)(2,1)S(1)}, bf16[256,960]{0,1:T(8,128)(2,1)S(1)}, u32[]{:S(2)}, u32[]{:S(2)}) %collective-permute-start.3) | collective-permute-done | bytes 491552 | tf_op jit(solution)/shard_map/ppermute | solution.py:16
  87.2 5.8 collective-permute-start.4
  93.0 21.2 %collective-permute-done.4 = bf16[256,960]{0,1:T(8,128)(2,1)S(1)} collective-permute-done((bf16[256,960]{0,1:T(8,128)(2,1)S(1)}, bf16[256,960]{0,1:T(8,128)(2,1)S(1)}, u32[]{:S(2)}, u32[]{:S(2)}) %collective-permute-start.4) | collective-permute-done | bytes 491552 | tf_op jit(solution)/shard_map/ppermute | solution.py:16
  114.5 8.2 collective-permute-start.5
  122.7 19.2 %collective-permute-done.5 = bf16[256,960]{0,1:T(8,128)(2,1)S(1)} collective-permute-done((bf16[256,960]{0,1:T(8,128)(2,1)S(1)}, bf16[256,960]{0,1:T(8,128)(2,1)S(1)}, u32[]{:S(2)}, u32[]{:S(2)}) %collective-permute-start.5) | collective-permute-done | bytes 491552 | tf_op jit(solution)/shard_map/ppermute | solution.py:16
  144.1 9.0 collective-permute-done.6
  153.3 4.7 collective-permute-start.7
  158.1 21.2 %collective-permute-done.7 = bf16[256,960]{0,1:T(8,128)(2,1)S(1)} collective-permute-done((bf16[256,960]{0,1:T(8,128)(2,1)S(1)}, bf16[256,960]{0,1:T(8,128)(2,1)S(1)}, u32[]{:S(2)}, u32[]{:S(2)}) %collective-permute-start.7) | collective-permute-done | bytes 491552 | tf_op jit(solution)/shard_map/ppermute | solution.py:16
  179.5 4.6 collective-permute-start.8
  184.1 24.5 %collective-permute-done.8 = bf16[256,960]{0,1:T(8,128)(2,1)S(1)} collective-permute-done((bf16[256,960]{0,1:T(8,128)(2,1)S(1)}, bf16[256,960]{0,1:T(8,128)(2,1)S(1)}, u32[]{:S(2)}, u32[]{:S(2)}) %collective-permute-start.8) | collective-permute-done | bytes 491552 | tf_op jit(solution)/shard_map/ppermute | solution.py:16
  208.8 4.4 collective-permute-start.9
  213.2 11.1 %collective-permute-done.9 = bf16[256,960]{0,1:T(8,128)(2,1)S(1)} collective-permute-done((bf16[256,960]{0,1:T(8,128)(2,1)S(1)}, bf16[256,960]{0,1:T(8,128)(2,1)S(1)}, u32[]{:S(2)}, u32[]{:S(2)}) %collective-permute-start.9) | collective-permute-done | bytes 491552 | tf_op jit(solution)/shard_map/ppermute | solution.py:16
  224.5 9.0 collective-permute-start.10
  233.5 21.3 %collective-permute-done.10 = bf16[256,960]{0,1:T(8,128)(2,1)S(1)} collective-permute-done((bf16[256,960]{0,1:T(8,128)(2,1)S(1)}, bf16[256,960]{0,1:T(8,128)(2,1)S(1)}, u32[]{:S(2)}, u32[]{:S(2)}) %collective-permute-start.10) | collective-permute-done | bytes 491552 | tf_op jit(solution)/shard_map/ppermute | solution.py:16
  255.0 3.8 collective-permute-start.11
  263.7 19.4 %collective-permute-done.11 = bf16[256,960]{0,1:T(8,128)(2,1)} collective-permute-done((bf16[256,960]{0,1:T(8,128)(2,1)S(1)}, bf16[256,960]{0,1:T(8,128)(2,1)}, u32[]{:S(2)}, u32[]{:S(2)}) %collective-permute-start.11) | collective-permute-done | bytes 491552 | tf_op jit(solution)/shard_map/ppermute | solution.py:16
  296.7 4.8 collective-permute-start.13
  301.6 4.6 collective-permute-start.12
  306.1 8.5 collective-permute-done.12
  316.7 4.3 collective-permute-start.14
  321.0 18.3 %collective-permute-done.14 = bf16[256,1]{0,1:T(2,128)(2,1)S(1)} collective-permute-done((bf16[256,1]{0,1:T(2,128)(2,1)S(1)}, bf16[256,1]{0,1:T(2,128)(2,1)S(1)}, u32[]{:S(2)}, u32[]{:S(2)}) %collective-permute-start.14) | collective-permute-done | bytes 544 | tf_op jit(solution)/shard_map/ppermute | solution.py:16
  344.8 6.7 collective-permute-done.16
  351.7 4.7 collective-permute-start.19
  356.4 4.5 collective-permute-start.18
  360.9 5.8 collective-permute-done.18
  368.8 4.3 collective-permute-start.20
  373.1 18.5 %collective-permute-done.20 = bf16[256,1]{0,1:T(2,128)(2,1)S(1)} collective-permute-done((bf16[256,1]{0,1:T(2,128)(2,1)S(1)}, bf16[256,1]{0,1:T(2,128)(2,1)S(1)}, u32[]{:S(2)}, u32[]{:S(2)}) %collective-permute-start.20) | collective-permute-done | bytes 544 | tf_op jit(solution)/shard_map/ppermute | solution.py:16
  397.1 6.6 collective-permute-done.22
  405.1 4.2 collective-permute-start.25
  409.3 5.0 collective-permute-start.24
  414.3 5.7 collective-permute-done.24
  420.2 18.7 %collective-permute-start.27 = (bf16[256,960]{0,1:T(8,128)(2,1)S(1)}, bf16[256,960]{0,1:T(8,128)(2,1)S(1)}, u32[]{:S(2)}, u32[]{:S(2)}) collective-permute-start(bf16[256,960]{0,1:T(8,128)(2,1)S(1)} %add_convert_fusion.5), channel_id=1, source_target_pairs={{0,16},{1,17},{2,18},{3,19},{4,20},{5,21},{6,22},{7,23},{8,24},{9,... | collective-permute-start | bytes 1474568 | tf_op jit(solution)/shard_map/ppermute | solution.py:16
  440.8 19.7 %collective-permute-done.26 = bf16[256,1]{0,1:T(2,128)(2,1)S(1)} collective-permute-done((bf16[256,1]{0,1:T(2,128)(2,1)S(1)}, bf16[256,1]{0,1:T(2,128)(2,1)S(1)}, u32[]{:S(2)}, u32[]{:S(2)}) %collective-permute-start.26) | collective-permute-done | bytes 544 | tf_op jit(solution)/shard_map/ppermute | solution.py:16
  466.0 4.6 collective-permute-start.30
  470.7 3.5 collective-permute-done.28
  475.2 4.6 collective-permute-start.31
  486.5 4.7 collective-permute-done.31
  492.6 17.7 %collective-permute-start.33 = (bf16[256,960]{0,1:T(8,128)(2,1)S(1)}, bf16[256,960]{0,1:T(8,128)(2,1)}, u32[]{:S(2)}, u32[]{:S(2)}) collective-permute-start(bf16[256,960]{0,1:T(8,128)(2,1)S(1)} %add_convert_fusion.2), channel_id=1, source_target_pairs={{0,2},{1,3},{2,0},{3,1},{4,6},{5,7},{6,4},{7,5},{8,10},{9,11},{10,... | collective-permute-start | bytes 1474568 | tf_op jit(solution)/shard_map/ppermute | solution.py:16
  510.4 155.1 %fusion.38 = (f32[240,32]{0,1:T(8,128)S(1)}, f32[240,32]{0,1:T(8,128)S(1)}) fusion(f32[240,1920]{0,1:T(8,128)S(1)} %bitcast.155, f32[240,1920]{0,1:T(8,128)} %bitcast.156), kind=kCustom, calls=%all-reduce-scatter.2 | all-reduce-scatter fusion | flops 983041 | bytes 3749888
  682.5 111.8 %all-reduce.2 = f32[1,960]{1,0:T(1,128)S(1)} all-reduce(f32[1,960]{1,0:T(1,128)S(1)} %bitcast.161), channel_id=4, replica_groups=mesh['dp'=8,'seq'=64] {'seq'}, use_global_device_ids=true, to_apply=%region_8.0.clone | all-reduce | flops 960 | bytes 7680
  806.0 107.8 %all-reduce.8 = (bf16[256,960]{0,1:T(8,128)(2,1)}, f32[240,30]{0,1:T(8,128)S(1)}, f32[240,30]{0,1:T(8,128)S(1)}, f32[1,15]{1,0:T(1,128)S(1)}) all-reduce(f32[256,960]{0,1:T(8,128)S(1)} %copy-done.1, f32[240,30]{0,1:T(8,128)S(1)} %constant_dynamic-slice_fusion.1, ...), channel_id=1, replica_groups=mesh['dp'=8,'seq'=64] {'dp'}, use_global_device_ids=true, to_apply=%region_2.0 | all-reduce | flops 260175 | bytes 1589880 | tf_op jit(solution)/shard_map/psum | solution.py:136
  (155 shorter events, 88.6 us)
Async XLA Ops:
  0.6 283.8 %copy-start = (bf16[256,256]{1,0:T(8,128)(2,1)S(1)}, bf16[256,256]{1,0:T(8,128)(2,1)}, u32[]{:S(2)}) copy-start(bf16[256,256]{1,0:T(8,128)(2,1)} %param.14) | copy-start | bytes 393220
  2.1 10.3 %collective-permute-start = (bf16[256,960]{0,1:T(8,128)(2,1)S(1)}, bf16[256,960]{0,1:T(8,128)(2,1)S(1)}, u32[]{:S(2)}, u32[]{:S(2)}) collective-permute-start(bf16[256,960]{0,1:T(8,128)(2,1)S(1)} %convolution_convert_fusion.1), channel_id=1, source_target_pairs={{0,1},{1,0},{2,3},{3,2},{4,5},{5,4},{6,7},{7,6},{8,9},{9,8},{10,11... | collective-permute-start | bytes 1474568 | tf_op jit(solution)/shard_map/ppermute | solution.py:16
  12.5 29.9 %collective-permute-start.1 = (bf16[256,960]{0,1:T(8,128)(2,1)S(1)}, bf16[256,960]{0,1:T(8,128)(2,1)S(1)}, u32[]{:S(2)}, u32[]{:S(2)}) collective-permute-start(bf16[256,960]{0,1:T(8,128)(2,1)S(1)} %add_convert_fusion.23), channel_id=1, source_target_pairs={{0,2},{1,3},{2,0},{3,1},{4,6},{5,7},{6,4},{7,5},{8,10},{9,11},{10,... | collective-permute-start | bytes 1474568 | tf_op jit(solution)/shard_map/ppermute | solution.py:16
  42.6 30.0 %collective-permute-start.2 = (bf16[256,960]{0,1:T(8,128)(2,1)S(1)}, bf16[256,960]{0,1:T(8,128)(2,1)S(1)}, u32[]{:S(2)}, u32[]{:S(2)}) collective-permute-start(bf16[256,960]{0,1:T(8,128)(2,1)S(1)} %add_convert_fusion.22), channel_id=1, source_target_pairs={{0,4},{1,5},{2,6},{3,7},{4,0},{5,1},{6,2},{7,3},{8,12},{9,13},{10,... | collective-permute-start | bytes 1474568 | tf_op jit(solution)/shard_map/ppermute | solution.py:16
  72.9 14.1 %collective-permute-start.3 = (bf16[256,960]{0,1:T(8,128)(2,1)S(1)}, bf16[256,960]{0,1:T(8,128)(2,1)S(1)}, u32[]{:S(2)}, u32[]{:S(2)}) collective-permute-start(bf16[256,960]{0,1:T(8,128)(2,1)S(1)} %add_convert_fusion.21), channel_id=1, source_target_pairs={{0,8},{1,9},{2,10},{3,11},{4,12},{5,13},{6,14},{7,15},{8,0},{9,1},... | collective-permute-start | bytes 1474568 | tf_op jit(solution)/shard_map/ppermute | solution.py:16
  87.2 27.0 %collective-permute-start.4 = (bf16[256,960]{0,1:T(8,128)(2,1)S(1)}, bf16[256,960]{0,1:T(8,128)(2,1)S(1)}, u32[]{:S(2)}, u32[]{:S(2)}) collective-permute-start(bf16[256,960]{0,1:T(8,128)(2,1)S(1)} %add_convert_fusion.20), channel_id=1, source_target_pairs={{0,16},{1,17},{2,18},{3,19},{4,20},{5,21},{6,22},{7,23},{8,24},{9,... | collective-permute-start | bytes 1474568 | tf_op jit(solution)/shard_map/ppermute | solution.py:16
  114.5 27.4 %collective-permute-start.5 = (bf16[256,960]{0,1:T(8,128)(2,1)S(1)}, bf16[256,960]{0,1:T(8,128)(2,1)S(1)}, u32[]{:S(2)}, u32[]{:S(2)}) collective-permute-start(bf16[256,960]{0,1:T(8,128)(2,1)S(1)} %add_convert_fusion.19), channel_id=1, source_target_pairs={{0,32},{1,33},{2,34},{3,35},{4,36},{5,37},{6,38},{7,39},{8,40},{9,... | collective-permute-start | bytes 1474568 | tf_op jit(solution)/shard_map/ppermute | solution.py:16
  142.2 10.9 %collective-permute-start.6 = (bf16[256,960]{0,1:T(8,128)(2,1)S(1)}, bf16[256,960]{0,1:T(8,128)(2,1)S(1)}, u32[]{:S(2)}, u32[]{:S(2)}) collective-permute-start(bf16[256,960]{0,1:T(8,128)(2,1)S(1)} %fusion.15), channel_id=1, source_target_pairs={{0,1},{1,0},{2,3},{3,2},{4,5},{5,4},{6,7},{7,6},{8,9},{9,8},{10,11... | collective-permute-start | bytes 1474568 | tf_op jit(solution)/shard_map/ppermute | solution.py:16
  153.3 26.0 %collective-permute-start.7 = (bf16[256,960]{0,1:T(8,128)(2,1)S(1)}, bf16[256,960]{0,1:T(8,128)(2,1)S(1)}, u32[]{:S(2)}, u32[]{:S(2)}) collective-permute-start(bf16[256,960]{0,1:T(8,128)(2,1)S(1)} %add_convert_fusion.17), channel_id=1, source_target_pairs={{0,2},{1,3},{2,0},{3,1},{4,6},{5,7},{6,4},{7,5},{8,10},{9,11},{10,... | collective-permute-start | bytes 1474568 | tf_op jit(solution)/shard_map/ppermute | solution.py:16
  179.5 29.1 %collective-permute-start.8 = (bf16[256,960]{0,1:T(8,128)(2,1)S(1)}, bf16[256,960]{0,1:T(8,128)(2,1)S(1)}, u32[]{:S(2)}, u32[]{:S(2)}) collective-permute-start(bf16[256,960]{0,1:T(8,128)(2,1)S(1)} %add_convert_fusion.16), channel_id=1, source_target_pairs={{0,4},{1,5},{2,6},{3,7},{4,0},{5,1},{6,2},{7,3},{8,12},{9,13},{10,... | collective-permute-start | bytes 1474568 | tf_op jit(solution)/shard_map/ppermute | solution.py:16
  208.8 15.6 %collective-permute-start.9 = (bf16[256,960]{0,1:T(8,128)(2,1)S(1)}, bf16[256,960]{0,1:T(8,128)(2,1)S(1)}, u32[]{:S(2)}, u32[]{:S(2)}) collective-permute-start(bf16[256,960]{0,1:T(8,128)(2,1)S(1)} %add_convert_fusion.15), channel_id=1, source_target_pairs={{0,8},{1,9},{2,10},{3,11},{4,12},{5,13},{6,14},{7,15},{8,0},{9,1},... | collective-permute-start | bytes 1474568 | tf_op jit(solution)/shard_map/ppermute | solution.py:16
  224.5 30.3 %collective-permute-start.10 = (bf16[256,960]{0,1:T(8,128)(2,1)S(1)}, bf16[256,960]{0,1:T(8,128)(2,1)S(1)}, u32[]{:S(2)}, u32[]{:S(2)}) collective-permute-start(bf16[256,960]{0,1:T(8,128)(2,1)S(1)} %add_convert_fusion.14), channel_id=1, source_target_pairs={{0,16},{1,17},{2,18},{3,19},{4,20},{5,21},{6,22},{7,23},{8,24},{9,... | collective-permute-start | bytes 1474568 | tf_op jit(solution)/shard_map/ppermute | solution.py:16
  255.0 28.1 %collective-permute-start.11 = (bf16[256,960]{0,1:T(8,128)(2,1)S(1)}, bf16[256,960]{0,1:T(8,128)(2,1)}, u32[]{:S(2)}, u32[]{:S(2)}) collective-permute-start(bf16[256,960]{0,1:T(8,128)(2,1)S(1)} %add_convert_fusion.13), channel_id=1, source_target_pairs={{0,32},{1,33},{2,34},{3,35},{4,36},{5,37},{6,38},{7,39},{8,40},{9,... | collective-permute-start | bytes 1474568 | tf_op jit(solution)/shard_map/ppermute | solution.py:16
  296.7 17.9 %collective-permute-start.13 = (bf16[256,960]{0,1:T(8,128)(2,1)S(1)}, bf16[256,960]{0,1:T(8,128)(2,1)S(1)}, u32[]{:S(2)}, u32[]{:S(2)}) collective-permute-start(bf16[256,960]{0,1:T(8,128)(2,1)S(1)} %fusion.13), channel_id=1, source_target_pairs={{0,32},{1,33},{2,34},{3,35},{4,36},{5,37},{6,38},{7,39},{8,40},{9,... | collective-permute-start | bytes 1474568 | tf_op jit(solution)/shard_map/ppermute | solution.py:16
  301.6 13.1 %collective-permute-start.12 = (bf16[256,1]{0,1:T(2,128)(2,1)S(1)}, bf16[256,1]{0,1:T(2,128)(2,1)S(1)}, u32[]{:S(2)}, u32[]{:S(2)}) collective-permute-start(bf16[256,1]{0,1:T(2,128)(2,1)S(1)} %get-tuple-element.31), channel_id=1, source_target_pairs={{0,32},{1,33},{2,34},{3,35},{4,36},{5,37},{6,38},{7,39},{8,40},{9,... | collective-permute-start | bytes 1544 | tf_op jit(solution)/shard_map/ppermute | solution.py:16
  314.8 24.5 %collective-permute-start.15 = (bf16[256,960]{0,1:T(8,128)(2,1)S(1)}, bf16[256,960]{0,1:T(8,128)(2,1)S(1)}, u32[]{:S(2)}, u32[]{:S(2)}) collective-permute-start(bf16[256,960]{0,1:T(8,128)(2,1)S(1)} %add_convert_fusion.11), channel_id=1, source_target_pairs={{0,16},{1,17},{2,18},{3,19},{4,20},{5,21},{6,22},{7,23},{8,24},{9,... | collective-permute-start | bytes 1474568 | tf_op jit(solution)/shard_map/ppermute | solution.py:16
  316.7 22.5 %collective-permute-start.14 = (bf16[256,1]{0,1:T(2,128)(2,1)S(1)}, bf16[256,1]{0,1:T(2,128)(2,1)S(1)}, u32[]{:S(2)}, u32[]{:S(2)}) collective-permute-start(bf16[256,1]{0,1:T(2,128)(2,1)S(1)} %get-tuple-element.30), channel_id=1, source_target_pairs={{0,16},{1,17},{2,18},{3,19},{4,20},{5,21},{6,22},{7,23},{8,24},{9,... | collective-permute-start | bytes 1544 | tf_op jit(solution)/shard_map/ppermute | solution.py:16
  339.5 12.0 %collective-permute-start.17 = (bf16[256,960]{0,1:T(8,128)(2,1)S(1)}, bf16[256,960]{0,1:T(8,128)(2,1)S(1)}, u32[]{:S(2)}, u32[]{:S(2)}) collective-permute-start(bf16[256,960]{0,1:T(8,128)(2,1)S(1)} %add_convert_fusion.10), channel_id=1, source_target_pairs={{0,8},{1,9},{2,10},{3,11},{4,12},{5,13},{6,14},{7,15},{8,0},{9,1},... | collective-permute-start | bytes 1474568 | tf_op jit(solution)/shard_map/ppermute | solution.py:16
  341.5 10.0 %collective-permute-start.16 = (bf16[256,1]{0,1:T(2,128)(2,1)S(1)}, bf16[256,1]{0,1:T(2,128)(2,1)S(1)}, u32[]{:S(2)}, u32[]{:S(2)}) collective-permute-start(bf16[256,1]{0,1:T(2,128)(2,1)S(1)} %get-tuple-element.29), channel_id=1, source_target_pairs={{0,8},{1,9},{2,10},{3,11},{4,12},{5,13},{6,14},{7,15},{8,0},{9,1},... | collective-permute-start | bytes 1544 | tf_op jit(solution)/shard_map/ppermute | solution.py:16
  351.7 15.0 %collective-permute-start.19 = (bf16[256,960]{0,1:T(8,128)(2,1)S(1)}, bf16[256,960]{0,1:T(8,128)(2,1)S(1)}, u32[]{:S(2)}, u32[]{:S(2)}) collective-permute-start(bf16[256,960]{0,1:T(8,128)(2,1)S(1)} %add_convert_fusion.9), channel_id=1, source_target_pairs={{0,4},{1,5},{2,6},{3,7},{4,0},{5,1},{6,2},{7,3},{8,12},{9,13},{10,... | collective-permute-start | bytes 1474568 | tf_op jit(solution)/shard_map/ppermute | solution.py:16
  356.4 10.3 %collective-permute-start.18 = (bf16[256,1]{0,1:T(2,128)(2,1)S(1)}, bf16[256,1]{0,1:T(2,128)(2,1)S(1)}, u32[]{:S(2)}, u32[]{:S(2)}) collective-permute-start(bf16[256,1]{0,1:T(2,128)(2,1)S(1)} %get-tuple-element.28), channel_id=1, source_target_pairs={{0,4},{1,5},{2,6},{3,7},{4,0},{5,1},{6,2},{7,3},{8,12},{9,13},{10,... | collective-permute-start | bytes 1544 | tf_op jit(solution)/shard_map/ppermute | solution.py:16
  366.9 24.7 %collective-permute-start.21 = (bf16[256,960]{0,1:T(8,128)(2,1)S(1)}, bf16[256,960]{0,1:T(8,128)(2,1)S(1)}, u32[]{:S(2)}, u32[]{:S(2)}) collective-permute-start(bf16[256,960]{0,1:T(8,128)(2,1)S(1)} %add_convert_fusion.8), channel_id=1, source_target_pairs={{0,2},{1,3},{2,0},{3,1},{4,6},{5,7},{6,4},{7,5},{8,10},{9,11},{10,... | collective-permute-start | bytes 1474568 | tf_op jit(solution)/shard_map/ppermute | solution.py:16
  368.8 22.8 %collective-permute-start.20 = (bf16[256,1]{0,1:T(2,128)(2,1)S(1)}, bf16[256,1]{0,1:T(2,128)(2,1)S(1)}, u32[]{:S(2)}, u32[]{:S(2)}) collective-permute-start(bf16[256,1]{0,1:T(2,128)(2,1)S(1)} %get-tuple-element.27), channel_id=1, source_target_pairs={{0,2},{1,3},{2,0},{3,1},{4,6},{5,7},{6,4},{7,5},{8,10},{9,11},{10,... | collective-permute-start | bytes 1544 | tf_op jit(solution)/shard_map/ppermute | solution.py:16
  391.8 11.9 %collective-permute-start.23 = (bf16[256,960]{0,1:T(8,128)(2,1)S(1)}, bf16[256,960]{0,1:T(8,128)(2,1)S(1)}, u32[]{:S(2)}, u32[]{:S(2)}) collective-permute-start(bf16[256,960]{0,1:T(8,128)(2,1)S(1)} %add_convert_fusion.7), channel_id=1, source_target_pairs={{0,1},{1,0},{2,3},{3,2},{4,5},{5,4},{6,7},{7,6},{8,9},{9,8},{10,11... | collective-permute-start | bytes 1474568 | tf_op jit(solution)/shard_map/ppermute | solution.py:16
  393.7 10.0 %collective-permute-start.22 = (bf16[256,1]{0,1:T(2,128)(2,1)S(1)}, bf16[256,1]{0,1:T(2,128)(2,1)S(1)}, u32[]{:S(2)}, u32[]{:S(2)}) collective-permute-start(bf16[256,1]{0,1:T(2,128)(2,1)S(1)} %get-tuple-element.26), channel_id=1, source_target_pairs={{0,1},{1,0},{2,3},{3,2},{4,5},{5,4},{6,7},{7,6},{8,9},{9,8},{10,11... | collective-permute-start | bytes 1544 | tf_op jit(solution)/shard_map/ppermute | solution.py:16
  405.1 14.9 %collective-permute-start.25 = (bf16[256,960]{0,1:T(8,128)(2,1)S(1)}, bf16[256,960]{0,1:T(8,128)(2,1)S(1)}, u32[]{:S(2)}, u32[]{:S(2)}) collective-permute-start(bf16[256,960]{0,1:T(8,128)(2,1)S(1)} %get-tuple-element.17), channel_id=1, source_target_pairs={{0,32},{1,33},{2,34},{3,35},{4,36},{5,37},{6,38},{7,39},{8,40},{9,... | collective-permute-start | bytes 1474568 | tf_op jit(solution)/shard_map/ppermute | solution.py:16
  409.3 10.7 %collective-permute-start.24 = (bf16[256,1]{0,1:T(2,128)(2,1)S(1)}, bf16[256,1]{0,1:T(2,128)(2,1)S(1)}, u32[]{:S(2)}, u32[]{:S(2)}) collective-permute-start(bf16[256,1]{0,1:T(2,128)(2,1)S(1)} %get-tuple-element.25), channel_id=1, source_target_pairs={{0,32},{1,33},{2,34},{3,35},{4,36},{5,37},{6,38},{7,39},{8,40},{9,... | collective-permute-start | bytes 1544 | tf_op jit(solution)/shard_map/ppermute | solution.py:16
  420.2 40.3 %collective-permute-start.27 = (bf16[256,960]{0,1:T(8,128)(2,1)S(1)}, bf16[256,960]{0,1:T(8,128)(2,1)S(1)}, u32[]{:S(2)}, u32[]{:S(2)}) collective-permute-start(bf16[256,960]{0,1:T(8,128)(2,1)S(1)} %add_convert_fusion.5), channel_id=1, source_target_pairs={{0,16},{1,17},{2,18},{3,19},{4,20},{5,21},{6,22},{7,23},{8,24},{9,... | collective-permute-start | bytes 1474568 | tf_op jit(solution)/shard_map/ppermute | solution.py:16
  438.9 21.6 %collective-permute-start.26 = (bf16[256,1]{0,1:T(2,128)(2,1)S(1)}, bf16[256,1]{0,1:T(2,128)(2,1)S(1)}, u32[]{:S(2)}, u32[]{:S(2)}) collective-permute-start(bf16[256,1]{0,1:T(2,128)(2,1)S(1)} %get-tuple-element.24), channel_id=1, source_target_pairs={{0,16},{1,17},{2,18},{3,19},{4,20},{5,21},{6,22},{7,23},{8,24},{9,... | collective-permute-start | bytes 1544 | tf_op jit(solution)/shard_map/ppermute | solution.py:16
  460.7 13.5 %collective-permute-start.29 = (bf16[256,960]{0,1:T(8,128)(2,1)S(1)}, bf16[256,960]{0,1:T(8,128)(2,1)S(1)}, u32[]{:S(2)}, u32[]{:S(2)}) collective-permute-start(bf16[256,960]{0,1:T(8,128)(2,1)S(1)} %add_convert_fusion.4), channel_id=1, source_target_pairs={{0,8},{1,9},{2,10},{3,11},{4,12},{5,13},{6,14},{7,15},{8,0},{9,1},... | collective-permute-start | bytes 1474568 | tf_op jit(solution)/shard_map/ppermute | solution.py:16
  463.7 10.5 %collective-permute-start.28 = (bf16[256,1]{0,1:T(2,128)(2,1)S(1)}, bf16[256,1]{0,1:T(2,128)(2,1)S(1)}, u32[]{:S(2)}, u32[]{:S(2)}) collective-permute-start(bf16[256,1]{0,1:T(2,128)(2,1)S(1)} %get-tuple-element.23), channel_id=1, source_target_pairs={{0,8},{1,9},{2,10},{3,11},{4,12},{5,13},{6,14},{7,15},{8,0},{9,1},... | collective-permute-start | bytes 1544 | tf_op jit(solution)/shard_map/ppermute | solution.py:16
  466.0 8.2 collective-permute-start.30
  475.2 16.0 %collective-permute-start.31 = (bf16[256,960]{0,1:T(8,128)(2,1)}, bf16[256,960]{0,1:T(8,128)(2,1)}, u32[]{:S(2)}, u32[]{:S(2)}) collective-permute-start(bf16[256,960]{0,1:T(8,128)(2,1)} %add_convert_fusion.3), channel_id=1, source_target_pairs={{0,4},{1,5},{2,6},{3,7},{4,0},{5,1},{6,2},{7,3},{8,12},{9,13},{10,... | collective-permute-start | bytes 1474568 | tf_op jit(solution)/shard_map/ppermute | solution.py:16
  492.6 309.9 %collective-permute-start.33 = (bf16[256,960]{0,1:T(8,128)(2,1)S(1)}, bf16[256,960]{0,1:T(8,128)(2,1)}, u32[]{:S(2)}, u32[]{:S(2)}) collective-permute-start(bf16[256,960]{0,1:T(8,128)(2,1)S(1)} %add_convert_fusion.2), channel_id=1, source_target_pairs={{0,2},{1,3},{2,0},{3,1},{4,6},{5,7},{6,4},{7,5},{8,10},{9,11},{10,... | collective-permute-start | bytes 1474568 | tf_op jit(solution)/shard_map/ppermute | solution.py:16
  510.3 170.2 %copy-start.18 = (u32[512]{0:T(512)S(1)}, u32[512]{0:T(512)}, u32[]{:S(2)}) copy-start(u32[512]{0:T(512)} %constant.25) | copy-start | bytes 6148
  665.4 140.6 %copy-start.1 = (f32[256,960]{0,1:T(8,128)S(1)}, f32[256,960]{0,1:T(8,128)}, u32[]{:S(2)}) copy-start(f32[256,960]{0,1:T(8,128)} %get-tuple-element.16) | copy-start | bytes 2949124
  665.4 130.1 %collective-permute-start.38 = (f32[240,32]{0,1:T(8,128)S(1)}, f32[240,32]{0,1:T(8,128)S(1)}, u32[]{:S(2)}, u32[]{:S(2)}) collective-permute-start(f32[240,32]{0,1:T(8,128)S(1)} %get-tuple-element.14), channel_id=1, source_target_pairs={{0,3},{1,4},{2,5},{3,6},{4,7},{5,8},{6,9},{7,10},{8,11},{9,12},{10... | collective-permute-start | bytes 92168
  666.9 130.0 %collective-permute-start.37 = (f32[240,32]{0,1:T(8,128)S(1)}, f32[240,32]{0,1:T(8,128)S(1)}, u32[]{:S(2)}, u32[]{:S(2)}) collective-permute-start(f32[240,32]{0,1:T(8,128)S(1)} %get-tuple-element.14), channel_id=1, source_target_pairs={{0,2},{1,3},{2,4},{3,5},{4,6},{5,7},{6,8},{7,9},{8,10},{9,11},{10,... | collective-permute-start | bytes 92168
  668.2 131.4 %collective-permute-start.36 = (f32[240,32]{0,1:T(8,128)S(1)}, f32[240,32]{0,1:T(8,128)S(1)}, u32[]{:S(2)}, u32[]{:S(2)}) collective-permute-start(f32[240,32]{0,1:T(8,128)S(1)} %get-tuple-element.14), channel_id=1, source_target_pairs={{0,1},{1,2},{2,3},{3,4},{4,5},{5,6},{6,7},{7,8},{8,9},{9,10},{10,1... | collective-permute-start | bytes 92168
  669.5 5.2 collective-permute-start.32
  674.7 4.6 collective-permute-start.34
  679.3 115.0 %collective-permute-start.39 = (f32[240,30]{0,1:T(8,128)S(1)}, f32[240,30]{0,1:T(8,128)S(1)}, u32[]{:S(2)}, u32[]{:S(2)}) collective-permute-start(f32[240,30]{0,1:T(8,128)S(1)} %slice.176), channel_id=1, source_target_pairs={{0,4},{1,5},{2,6},{3,7},{4,8},{5,9},{6,10},{7,11},{8,12},{9,13},{1... | collective-permute-start | bytes 86408
  794.3 7.6 collective-permute-start.42
  795.6 6.3 collective-permute-start.41
  796.9 5.0 collective-permute-start.40
  799.5 2.3 collective-permute-start.43
  802.5 112.7 %copy-start.15 = (bf16[256,256]{1,0:T(8,128)(2,1)S(1)}, bf16[256,256]{1,0:T(8,128)(2,1)}, u32[]{:S(2)}) copy-start(bf16[256,256]{1,0:T(8,128)(2,1)} %param.13) | copy-start | bytes 393220
  803.7 111.3 %collective-permute-start.35 = (bf16[256,960]{0,1:T(8,128)(2,1)S(1)}, bf16[256,960]{0,1:T(8,128)(2,1)S(1)}, u32[]{:S(2)}, u32[]{:S(2)}) collective-permute-start(bf16[256,960]{0,1:T(8,128)(2,1)S(1)} %add_convert_fusion.1), channel_id=1, source_target_pairs={{0,1},{1,0},{2,3},{3,2},{4,5},{5,4},{6,7},{7,6},{8,9},{9,8},{10,11... | collective-permute-start | bytes 1474568 | tf_op jit(solution)/shard_map/ppermute | solution.py:16
  (15 other events, 381.2 us)
where the time goes:
time: 933 us; the launch traced here: 916 us
  blocking collectives  375 us (40%)
  waiting for transfers between devices  309 us (33%)
  starting transfers between devices  189 us (20%)
  other arithmetic  16.1 us (2%)
  local copies, waits for them, and re-layouts  13.6 us (1%)
  matrix products  11 us (1%)
    ppermute x36, waiting for transfers between devices, swapped(): return lax.ppermute(value, axis, pairs)  309 us
    unnamed x2, blocking collectives  267 us
    ppermute x36, starting transfers between devices, swapped(): return lax.ppermute(value, axis, pairs)  177 us
    psum x1, blocking collectives, local(): lax.psum(spectrum.astype(jnp.float32) * weighted_grad.astype(jnp.float32)...  108 us
  transfers between devices with their start and end apart: 44, of which 26 were waited for; matrix products, arithmetic and copies ran while one was open for 19% of the time, Pallas kernels for 0%

commit v1 on v0

v1 whole, which is shorter than its diff:
```python
import jax
import jax.numpy as jnp
from jax import lax
from jax.experimental import pallas as pl
from jax.experimental.pallas import tpu as pltpu
from jax.sharding import PartitionSpec as P

MESH = pl.DeviceIdType.MESH
BF = jnp.bfloat16
F32 = jnp.float32

D = 960
GROUPS = 4
DG = 240
FFG = 480
SIDE = 8
PIECE = 16
ROOT_HALF = 0.7978845608028654
CUBIC = 0.044715
SCALE = 131072.0**-0.5
GAIN_WINDOWS = ((0, 256), (128, 512), (384, 768), (640, 960))
HIDDEN_WINDOWS = ((0, 512), (384, 1024), (896, 1536), (1408, 1920))


def dot(a, b):
    return lax.dot_general(a, b, (((1,), (0,)), ((), ())), preferred_element_type=F32)


def dot_tn(a, b):
    return lax.dot_general(a, b, (((0,), (0,)), ((), ())), preferred_element_type=F32)


def dot_nt(a, b):
    return lax.dot_general(a, b, (((1,), (1,)), ((), ())), preferred_element_type=F32)


def iotas(shape):
    return lax.broadcasted_iota(jnp.int32, shape, 0), lax.broadcasted_iota(jnp.int32, shape, 1)


def ones_where(mask):
    return jnp.where(mask, 1.0, 0.0).astype(BF)


def repeat(count, body, start=0):
    def step(index, carry):
        body(index)
        return carry

    lax.fori_loop(start, count, step, 0)


def wrapped(value):
    return lax.rem(value + 2 * SIDE, SIDE)


def await_bytes(view, sem):
    pltpu.make_async_copy(view, view, sem).wait()


def mix(values, selfs, crosses, bits, transposed):
    for k, bit in bits:
        stride = 1 << bit
        if transposed:
            scaled = [crosses[a][k] * values[a] for a in range(SIDE)]
            values = [selfs[a][k] * values[a] + scaled[a ^ stride] for a in range(SIDE)]
        else:
            values = [selfs[a][k] * values[a] + crosses[a][k] * values[a ^ stride] for a in range(SIDE)]
    return values


def kernel(
    x_hbm, cot_hbm, ker_hbm, min_hbm, mout_hbm, ts_hbm, tc_hbm, gain_hbm, up_hbm, down_hbm,
    out_hbm, ig_hbm, kg_hbm, ug_hbm, dg_hbm, gn_hbm,
    xv, kv, cotv, min_ref, mout_ref, ts_ref, tc_ref, gain_ref, up_ref, down_ref,
    outv, igv, kgv, ugv, dgv, gnv,
    eye, mint, moutt, twp, xg, cotg, cotn, upp, dnp, ww, acot, pa, act, pgr, hg, ng, ngr, hgr, acc, gaing, rowscale, wsum,
    src1, a1, ks, kt, ff, sp, src2, m2, src3, a3, src4, m4,
    kgb, kra, kgh, krb, kgs, kgf, gg, r1a, h1, r1b, fin, rf,
    in_s, out_s, s1, v1, s2, v2, s3, v3, s4, v4,
    ks_s, ks_v, ka_s, ka_v, kb_s, kb_v, kr_s, kr_v, kc_s, kc_v, kf_s, kf_v, kh_s, kh_v, ki_s, ki_v,
    ga_s, ga_v, gb_s, gb_v, gf_s, gf_v,
):
    loads = []

    def load(src, dst):
        copy = pltpu.make_async_copy(src, dst, in_s.at[len(loads)])
        copy.start()
        loads.append(copy)
        return copy

    def load_groups(src, dst):
        return [load(src.at[pl.ds(g * DG, DG)], dst.at[g, pl.ds(0, DG)]) for g in range(GROUPS)]

    tw_here = [load(ts_hbm, ts_ref), load(tc_hbm, tc_ref)]
    ker_here = load_groups(ker_hbm, kv)
    x_here = [load(min_hbm, min_ref)] + load_groups(x_hbm, xv)
    rest_here = load_groups(cot_hbm, cotv)
    rest_here += [load(gain_hbm, gain_ref), load(up_hbm, up_ref), load(down_hbm, down_ref), load(mout_hbm, mout_ref)]

    me = lax.axis_index("seq")
    z, y = lax.div(me, SIDE), lax.rem(me, SIDE)
    i = lax.axis_index("dp")
    chip, core = lax.div(i, 2), lax.rem(i, 2)
    mate = i + 1 - 2 * core
    yo = wrapped(i - y)

    barrier = pltpu.get_barrier_semaphore()

    def greet_seq(step):
        pl.semaphore_signal(
            barrier, inc=1, device_id={"seq": lax.rem(me + step, 64)}, device_id_type=MESH
        )

    def greet_dp(step):
        pl.semaphore_signal(barrier, inc=1, device_id={"dp": wrapped(i + step)}, device_id_type=MESH)

    repeat(64, greet_seq, 1)
    repeat(8, greet_dp, 1)

    def send(src, dst, ssem, rsem, device):
        pltpu.make_async_remote_copy(
            src_ref=src, dst_ref=dst, send_sem=ssem, recv_sem=rsem, device_id=device, device_id_type=MESH
        ).start()

    def send_part(part, src, dst, ssem, rsem):
        def one(dz, dy):
            tz, ty = wrapped(z + dz), wrapped(y + dy)
            send(src(tz, ty), dst, ssem.at[dz], rsem, {"seq": tz * SIDE + ty})

        if part == 0:
            pltpu.make_async_copy(src(z, y), dst, rsem).start()
            one(4, 0)

        def pair(t):
            one(part, lax.rem(5 * t, SIDE))
            one((4, 7, 6, 5)[part], lax.rem(5 * t, SIDE))

        repeat(SIDE, pair, 1 if part == 0 else 0)

    def await_sent(buffer, ssem):
        await_bytes(buffer.at[0, pl.ds(0, 7)], ssem.at[0])
        for dz in range(1, SIDE):
            await_bytes(buffer.at[0], ssem.at[dz])

    def store_grouped(ref, g, value):
        split = value.reshape(SIDE, 2, PIECE, 256)
        ref[:, g, :, 0:256] = split[:, 0]
        ref[:, 4 + g, :, 0:256] = split[:, 1]

    def load_grouped(ref, g):
        return jnp.stack([ref[:, g, :, 0:256], ref[:, 4 + g, :, 0:256]], axis=1).reshape(256, 256)

    def slot(chip_at, core_at):
        return wrapped(2 * chip_at + core_at - y)

    def to_chips(buffer, ssem, rsem):
        send(buffer.at[yo], buffer.at[yo], ssem.at[0], rsem.at[0], {"dp": mate})

        def step_to(step):
            send(
                buffer.at[yo], buffer.at[yo], ssem.at[step], rsem.at[step],
                {"dp": 2 * lax.rem(chip + step, 4) + core},
            )

        repeat(4, step_to, 1)

    def to_mate(buffer, rsem, ssem2, rsem2):
        def step_to(step):
            held = buffer.at[slot(lax.rem(chip + 4 - step, 4), core)]
            await_bytes(held, rsem.at[step])
            send(held, held, ssem2.at[step], rsem2.at[step], {"dp": mate})

        repeat(4, step_to, 1)

    def from_mate(buffer, rsem, rsem2):
        await_bytes(buffer.at[slot(chip, 1 - core)], rsem.at[0])

        def step_from(step):
            await_bytes(buffer.at[slot(lax.rem(chip + 4 - step, 4), 1 - core)], rsem2.at[step])

        repeat(4, step_from, 1)

    r, l = iotas((256, 256))
    eye[...] = ones_where(r == l)
    twp[...] = jnp.zeros_like(twp)
    for copy in tw_here:
        copy.wait()
    for k in range(6):
        for which in range(2):
            twp[which, pl.ds(DG + k, 1)] = ts_ref[k, which : which + 1].astype(F32)
            twp[which, pl.ds(DG + 8 + k, 1)] = tc_ref[k, which : which + 1].astype(F32)
    for copy in ker_here:
        copy.wait()
    for g in range(GROUPS):
        kv[g, pl.ds(DG, PIECE)] = twp[1, pl.ds(DG, PIECE)].astype(BF)
        store_grouped(ks, g, dot_nt(eye[...], kv[g]).astype(BF))
    columns = dot_nt(eye[...], twp[0].astype(BF))
    for copy in x_here:
        copy.wait()
    for g in range(GROUPS):
        xv[g, pl.ds(DG, PIECE)] = jnp.zeros((PIECE, 256), BF)
        store_grouped(src1, g, (dot_nt(min_ref[...], xv[g]) + columns).astype(BF))

    pl.semaphore_wait(barrier, 70)

    def share_kernel(dz):
        tz = wrapped(z + dz)
        send(ks.at[tz, yo], kt.at[y, z], ks_s.at[1], ks_v, {"seq": tz * SIDE + yo})

    repeat(SIDE, share_kernel, 1)

    @pl.when(yo != y)
    def _():
        send(ks.at[z, yo], kt.at[y, z], ks_s.at[0], ks_v, {"seq": z * SIDE + yo})

    @pl.when(yo == y)
    def _():
        pltpu.make_async_copy(ks.at[z, yo], kt.at[y, z], ks_v).start()

    first = (lambda tz, ty: src1.at[tz, ty], a1.at[z, y], s1, v1.at[z])
    send_part(0, *first)
    send_part(1, *first)
    await_bytes(kt.at[yo], ks_v)
    to_chips(kt, ka_s, ka_v)
    send_part(2, *first)
    send_part(3, *first)

    for copy in rest_here:
        copy.wait()
    for g in range(GROUPS):
        xg[g] = dot_nt(eye[...], xv[g]).astype(BF)
        cotv[g, pl.ds(DG, PIECE)] = jnp.zeros((PIECE, 256), BF)
    mint[...] = dot_nt(eye[...], min_ref[...]).astype(BF)
    moutt[...] = dot_nt(eye[...], mout_ref[...]).astype(BF)
    for g in range(GROUPS):
        cotn[g] = dot_nt(eye[...], cotv[g]).astype(BF)
        picked = jnp.zeros((256, 256), F32)
        for part in range(GROUPS):
            j, lane = iotas((256, 256))
            picked = picked + dot(ones_where((part * DG + lane == 4 * j + g) & (lane < DG)), cotv[part])
        cotg[g] = dot_nt(eye[...], picked.astype(BF)).astype(BF)
        low, high = GAIN_WINDOWS[g]
        channel, lane = iotas((high - low, 256))
        gain_rows = jnp.broadcast_to(gain_ref[:, low:high].astype(F32), (PIECE, high - low)).astype(BF)
        gaing[g] = dot(gain_rows, ones_where((channel + low == g * DG + lane) & (lane < DG)))[0:8]
    to_mate(kt, ka_v, kb_s, kb_v)
    for g in range(GROUPS):
        low, high = HIDDEN_WINDOWS[g]
        column, hidden_unit = iotas((high - low, 512))
        chosen = (column + low == g * FFG + hidden_unit - 2 * (hidden_unit >> 5)) & ((hidden_unit & 31) < 30)
        chooser = ones_where(chosen)
        upp[g, 0:DG] = dot(up_ref[:, low:high], chooser).astype(BF)
        dnp[g, 0:DG] = dot(down_ref[:, low:high], chooser).astype(BF)
        upp[g, DG:256] = jnp.zeros((256 - DG, 512), BF)
        dnp[g, DG:256] = jnp.zeros((256 - DG, 512), BF)

    def twiddles(slab):
        wide = slab.astype(F32)
        return [wide[:, 112 + k : 113 + k] for k in range(6)], [wide[:, 120 + k : 121 + k] for k in range(6)]

    def input_twiddles(shards):
        pairs = [twiddles(a1[sz, sy, :, 128:256]) for sz, sy in shards]
        return [p[0] for p in pairs], [p[1] for p in pairs]

    def output_twiddles(shards):
        pairs = [twiddles(kt[sy, sz, :, 128:256]) for sz, sy in shards]
        return [p[0] for p in pairs], [p[1] for p in pairs]

    low_bits = ((0, 0), (1, 1), (2, 2))
    high_bits = ((3, 0), (4, 1), (5, 2))
    low_back = tuple(reversed(low_bits))
    high_back = tuple(reversed(high_bits))

    def row_of(sz):
        return [(sz, a) for a in range(SIDE)]

    def column_of(sy):
        return [(a, sy) for a in range(SIDE)]

    def forward_one(step):
        sz = wrapped(z + step)
        await_bytes(a1.at[sz], v1.at[sz])
        shards = row_of(sz)
        values = [a1[p, q].astype(F32) for p, q in shards]
        values = mix(values, *input_twiddles(shards), low_bits, False)
        for (p, q), value in zip(shards, values):
            ff[p, q] = value

    repeat(SIDE, forward_one)
    from_mate(kt, ka_v, kb_v)

    def forward_two(sy):
        shards = column_of(sy)
        values = mix([ff[p, q] for p, q in shards], *input_twiddles(shards), high_bits, False)
        for (p, q), value in zip(shards, values):
            rounded = value.astype(BF)
            sp[p, q] = rounded
            ff[p, q] = rounded.astype(F32) * kt[q, p].astype(F32)

    repeat(SIDE, forward_two)

    def forward_three(sz):
        shards = row_of(sz)
        values = mix([ff[p, q] for p, q in shards], *output_twiddles(shards), low_bits, False)
        for (p, q), value in zip(shards, values):
            ff[p, q] = value

    repeat(SIDE, forward_three)

    def forward_four(sy):
        shards = column_of(sy)
        values = mix([ff[p, q] for p, q in shards], *output_twiddles(shards), high_bits, False)
        for (p, q), value in zip(shards, values):
            src2[p, q] = value.astype(BF)

    repeat(SIDE, forward_four)
    for part in range(4):
        send_part(part, lambda tz, ty: src2.at[tz, ty], m2.at[z, y], s2, v2.at[z])

    for g in range(GROUPS):
        acot[g] = dot(cotg[g], dnp[g])
        channel, j = iotas((D, 256))
        spread = ones_where((channel == 4 * j + g) & (j < DG))
        ww[:, pl.ds(g * 512, 512)] = dot(spread, dnp[g]).astype(BF)

    for sz in range(SIDE):
        await_bytes(m2.at[sz], v2.at[sz])

    lane_here = lax.broadcasted_iota(jnp.int32, (256, 256), 1) < DG
    squares = jnp.zeros((256, 1), F32)
    for g in range(GROUPS):
        value = xg[g].astype(F32) + dot(mout_ref[...], load_grouped(m2, g))
        value = jnp.where(lane_here, value, 0.0).astype(BF)
        hg[g] = value
        wide = value.astype(F32)
        squares = squares + jnp.sum(wide * wide, axis=1, keepdims=True)
    scale_column = lax.rsqrt(squares * (1.0 / D) + 1e-06)
    rowscale[...] = jnp.broadcast_to(scale_column, (256, 128))

    for g in range(GROUPS):
        wide = hg[g].astype(F32)
        ng[g] = (wide * rowscale[:, 0:1] * gaing[g, 0:1]).astype(BF)
        pa[...] = dot(ng[g], upp[g])

        def activate(tile, g=g):
            rows = pl.ds(pl.multiple_of(tile * 32, 32), 32)
            p = pa[rows]
            square = p * p
            tangent = jnp.tanh(p * (ROOT_HALF + (ROOT_HALF * CUBIC) * square))
            half_more = 0.5 + 0.5 * tangent
            act[rows, pl.ds(g * 512, 512)] = (p * half_more).astype(BF)
            inner = ROOT_HALF + (3.0 * ROOT_HALF * CUBIC) * square
            slope = half_more + 0.5 * p * (1.0 - tangent * tangent) * inner
            pgr[g, rows] = (acot[g, rows] * slope).astype(BF)

        repeat(8, activate)
        ngr[g] = dot_nt(pgr[g], upp[g])

    means = jnp.zeros((256, 1), F32)
    for g in range(GROUPS):
        means = means + jnp.sum(ngr[g] * gaing[g, 0:1] * hg[g].astype(F32), axis=1, keepdims=True)
    scale_column = rowscale[:, 0:1]
    means = means * (1.0 / D) * scale_column * scale_column * scale_column
    for g in range(GROUPS):
        gained = ngr[g] * gaing[g, 0:1]
        hgr[g] = (cotn[g].astype(F32) + scale_column * gained - hg[g].astype(F32) * means).astype(BF)
        store_grouped(src3, g, dot(moutt[...], hgr[g]).astype(BF))
    for part in range(4):
        send_part(part, lambda tz, ty: src3.at[tz, ty], a3.at[y, z], s3, v3.at[y])

    row_here = (lax.broadcasted_iota(jnp.int32, (512, 256), 0) & 31) == 30
    for g in range(GROUPS):
        gain_term = jnp.sum(ngr[g] * hg[g].astype(F32) * rowscale[:, 0:1], axis=0, keepdims=True)
        up_term = jnp.where(row_here, gain_term, dot_tn(pgr[g], ng[g]))
        down_term = dot_tn(act[:, pl.ds(g * 512, 512)], cotg[g])
        for kind, term in ((0, up_term), (1, down_term)):
            split = term.astype(BF).reshape(16, 2, PIECE, 256)
            for half in range(2):
                for side in range(2):
                    gg[side, 2 * kind + half, pl.ds(g * 16, 16)] = split[:, half, :, side * 128 : side * 128 + 128]

    send(gg.at[1 - core], r1a, ga_s, ga_v, {"dp": mate})

    acc[...] = dot_nt(ww[...], act[...])
    for g in range(GROUPS):
        rows = pl.ds(g * DG, DG)
        outv[rows] = (acc[rows] + dot_nt(eye[0:DG], hg[g])).astype(BF)
    pltpu.make_async_copy(outv, out_hbm, out_s.at[0]).start()

    await_bytes(r1a, ga_v)

    def pair_sum(step):
        for slab in range(4):
            part = pl.ds(pl.multiple_of(step * 8, 8), 8)
            both = gg[core, slab, part].astype(F32) + r1a[slab, part].astype(F32)
            h1[slab, part] = both.astype(BF)

    repeat(8, pair_sum)

    def spread_terms(step):
        other = lax.rem(chip + step, 4)
        send(h1.at[other], r1b.at[chip], gb_s.at[step], gb_v.at[step], {"dp": other * 2 + core})

    repeat(4, spread_terms, 1)

    def backward_one(step):
        sy = wrapped(y + step)
        await_bytes(a3.at[sy], v3.at[sy])
        shards = column_of(sy)
        values = [a3[q, p].astype(F32) for p, q in shards]
        values = mix(values, *output_twiddles(shards), high_back, True)
        for (p, q), value in zip(shards, values):
            ff[p, q] = value

    repeat(SIDE, backward_one)

    def backward_two(sz):
        shards = row_of(sz)
        values = mix([ff[p, q] for p, q in shards], *output_twiddles(shards), low_back, True)
        for (p, q), value in zip(shards, values):
            wide = value.astype(BF).astype(F32)
            owner = wrapped(q + y)
            kgb[lax.rem(owner, 2), lax.div(owner, 2), p] = (sp[p, q].astype(F32) * wide).astype(BF)
            ff[p, q] = wide * kt[q, p].astype(F32)

    repeat(SIDE, backward_two)

    send(kgb.at[1 - core], kra, kr_s, kr_v, {"dp": mate})

    def backward_three(sy):
        shards = column_of(sy)
        values = mix([ff[p, q] for p, q in shards], *input_twiddles(shards), high_back, True)
        for (p, q), value in zip(shards, values):
            ff[p, q] = value

    repeat(SIDE, backward_three)

    await_bytes(kra, kr_v)

    def kernel_pair(sz):
        for at in range(4):
            kgh[at, sz] = (kgb[core, at, sz].astype(F32) + kra[at, sz].astype(F32)).astype(BF)

    repeat(SIDE, kernel_pair)

    def spread_kernel_terms(step):
        other = lax.rem(chip + step, 4)
        send(kgh.at[other], krb.at[chip], kc_s.at[step], kc_v.at[step], {"dp": other * 2 + core})

    repeat(4, spread_kernel_terms, 1)

    def backward_four(sz):
        shards = row_of(sz)
        values = mix([ff[p, q] for p, q in shards], *input_twiddles(shards), low_back, True)
        for (p, q), value in zip(shards, values):
            src4[p, q, :, 0:256] = value.astype(BF)

    repeat(SIDE, backward_four)

    others = [lax.rem(chip + step, 4) for step in (1, 2, 3)]

    def terms_here(step):
        await_bytes(r1b.at[lax.rem(chip + 4 - step, 4)], gb_v.at[step])

    repeat(4, terms_here, 1)

    def chip_sum(sz):
        part = pl.ds(pl.multiple_of(sz * 8, 8), 8)
        four = h1[chip, part].astype(F32)
        for other in others:
            four = four + r1b[other, part].astype(F32)
        src4[sz, :, :, 256:384] = four.astype(BF)

    repeat(SIDE, chip_sum)

    last = (lambda tz, ty: src4.at[tz, ty], m4.at[z, y], s4, v4.at[z])
    send_part(0, *last)
    send_part(1, *last)

    def kernel_terms_here(step):
        await_bytes(krb.at[lax.rem(chip + 4 - step, 4)], kc_v.at[step])

    repeat(4, kernel_terms_here, 1)

    def kernel_sum(sz):
        four = kgh[chip, sz].astype(F32)
        for other in others:
            four = four + krb[other, sz].astype(F32)
        kgs[sz] = four.astype(BF)

    repeat(SIDE, kernel_sum)

    def return_kernel(dz):
        tz = wrapped(z + dz)
        send(kgs.at[tz], kgf.at[y, z], kf_s.at[1], kf_v, {"seq": tz * SIDE + yo})

    repeat(SIDE, return_kernel, 1)

    @pl.when(yo != y)
    def _():
        send(kgs.at[z], kgf.at[y, z], kf_s.at[0], kf_v, {"seq": z * SIDE + yo})

    @pl.when(yo == y)
    def _():
        pltpu.make_async_copy(kgs.at[z], kgf.at[y, z], kf_v).start()

    send_part(2, *last)
    send_part(3, *last)

    await_bytes(kgf.at[yo], kf_v)
    to_chips(kgf, kh_s, kh_v)
    to_mate(kgf, kh_v, ki_s, ki_v)
    from_mate(kgf, kh_v, ki_v)
    for g in range(GROUPS):
        held = jnp.stack([kgf[g], kgf[4 + g]], axis=1).reshape(256, 256)
        kgv[pl.ds(g * DG, DG)] = dot_nt(eye[0:DG], held).astype(BF)
    pltpu.make_async_copy(kgv, kg_hbm, out_s.at[1]).start()

    shard_sum = jnp.zeros((PIECE, 128), F32)
    for sz in range(SIDE):
        await_bytes(m4.at[sz], v4.at[sz])
        for sy in range(SIDE):
            shard_sum = shard_sum + m4[sz, sy, :, 256:384].astype(F32)
    shard_sum = shard_sum * SCALE
    fin[...] = shard_sum
    rf[i] = shard_sum

    def spread_grads(step):
        send(fin, rf.at[i], gf_s.at[step], gf_v.at[step], {"dp": wrapped(i + step)})

    repeat(SIDE, spread_grads, 1)

    for g in range(GROUPS):
        value = (hgr[g].astype(F32) + dot(mint[...], load_grouped(m4, g))).astype(BF)
        igv[pl.ds(g * DG, DG)] = dot_nt(eye[0:DG], value).astype(BF)
    pltpu.make_async_copy(igv, ig_hbm, out_s.at[2]).start()

    def grads_here(step):
        await_bytes(rf.at[wrapped(i - step)], gf_v.at[step])

    repeat(SIDE, grads_here, 1)
    for share in range(SIDE):
        kind, half, side = share // 4, (share // 2) % 2, share % 2
        wsum[kind, pl.ds(half * PIECE, PIECE), pl.ds(side * 128, 128)] = rf[share]
    ugv[...] = wsum[0, 0:30, 0:DG]
    dgv[...] = wsum[1, 0:30, 0:DG]
    j, lane = iotas((256, 128))
    picker = jnp.where(j == lane + 15 * lax.rem(me, 16), 1.0, 0.0)
    gains = jnp.broadcast_to(wsum[0, 30:31], (8, 256))
    picked = lax.dot_general(
        gains, picker, (((1,), (0,)), ((), ())), precision=lax.Precision.HIGHEST, preferred_element_type=F32
    )
    gnv[...] = picked[0:1, 0:15]
    pltpu.make_async_copy(ugv, ug_hbm, out_s.at[3]).start()
    pltpu.make_async_copy(dgv, dg_hbm, out_s.at[4]).start()
    pltpu.make_async_copy(gnv, gn_hbm, out_s.at[5]).start()

    for buffer, sem in ((src1, s1), (src2, s2), (src3, s3), (src4, s4)):
        await_sent(buffer, sem)
    await_bytes(ks.at[0, pl.ds(0, 7)], ks_s.at[1])
    await_bytes(kgs.at[pl.ds(0, 7)], kf_s.at[1])

    @pl.when(yo != y)
    def _():
        await_bytes(ks.at[0, 0], ks_s.at[0])
        await_bytes(kgs.at[0], kf_s.at[0])

    await_bytes(kt.at[0], ka_s.at[0])
    await_bytes(kgf.at[0], kh_s.at[0])
    await_bytes(r1a, ga_s)
    await_bytes(kra, kr_s)

    def chips_left(step):
        await_bytes(kt.at[0], ka_s.at[step])
        await_bytes(kt.at[0], kb_s.at[step])
        await_bytes(kgf.at[0], kh_s.at[step])
        await_bytes(kgf.at[0], ki_s.at[step])
        await_bytes(kgh.at[0], kc_s.at[step])
        await_bytes(h1.at[0], gb_s.at[step])

    repeat(4, chips_left, 1)

    def grads_left(step):
        await_bytes(fin, gf_s.at[step])

    repeat(SIDE, grads_left, 1)
    outs = ((outv, out_hbm), (kgv, kg_hbm), (igv, ig_hbm), (ugv, ug_hbm), (dgv, dg_hbm), (gnv, gn_hbm))
    for index, (held, there) in enumerate(outs):
        pltpu.make_async_copy(held, there, out_s.at[index]).wait()


def settle(*refs):
    held, there, sems = refs[:6], refs[6:12], refs[12]
    copies = [pltpu.make_async_copy(held[index], there[index], sems.at[index]) for index in range(6)]
    for copy in copies:
        copy.start()
    for copy in copies:
        copy.wait()


def local(
    inputs, cotangent, kernel_values, mix_in, mix_out, twiddle_self, twiddle_cross, norm_gain, up_weight, down_weight
):
    hbm = pl.BlockSpec(memory_space=pltpu.HBM)
    dma = pltpu.SemaphoreType.DMA
    vmem = pltpu.VMEM
    exchange = vmem((SIDE, SIDE, PIECE, 256), BF)
    longer = vmem((SIDE, SIDE, PIECE, 384), BF)
    grouped = vmem((GROUPS, 256, 256), BF)
    square = vmem((256, 256), BF)
    quarter = vmem((4, SIDE, PIECE, 256), BF)
    terms = vmem((4, 64, PIECE, 128), BF)
    wide = (D, 256)
    scratch = dict(
        xv=grouped, kv=grouped, cotv=grouped, min_ref=square, mout_ref=square,
        ts_ref=vmem((6, 2, 256), BF), tc_ref=vmem((6, 2, 256), BF), gain_ref=vmem((1, D), BF),
        up_ref=vmem((DG, 1920), BF), down_ref=vmem((DG, 1920), BF),
        outv=vmem(wide, BF), igv=vmem(wide, BF), kgv=vmem(wide, BF),
        ugv=vmem((30, DG), F32), dgv=vmem((30, DG), F32), gnv=vmem((1, 15), F32),
        eye=square, mint=square, moutt=square, twp=vmem((2, 256, 256), F32),
        xg=grouped, cotg=grouped, cotn=grouped,
        upp=vmem((GROUPS, 256, 512), BF), dnp=vmem((GROUPS, 256, 512), BF), ww=vmem((D, 2048), BF),
        acot=vmem((GROUPS, 256, 512), F32), pa=vmem((256, 512), F32), act=vmem((256, 2048), BF),
        pgr=vmem((GROUPS, 256, 512), BF), hg=grouped, ng=grouped, ngr=vmem((GROUPS, 256, 256), F32),
        hgr=grouped, acc=vmem(wide, F32), gaing=vmem((GROUPS, 8, 256), F32), rowscale=vmem((256, 128), F32),
        wsum=vmem((2, 32, 256), F32),
        src1=exchange, a1=exchange, ks=exchange, kt=exchange, ff=vmem((SIDE, SIDE, PIECE, 256), F32), sp=exchange,
        src2=exchange, m2=exchange, src3=exchange, a3=exchange, src4=longer, m4=longer,
        kgb=vmem((2, 4, SIDE, PIECE, 256), BF), kra=quarter, kgh=quarter, krb=quarter,
        kgs=vmem((SIDE, PIECE, 256), BF), kgf=exchange,
        gg=vmem((2, 4, 64, PIECE, 128), BF), r1a=terms, h1=terms, r1b=terms,
        fin=vmem((PIECE, 128), F32), rf=vmem((SIDE, PIECE, 128), F32),
        in_s=dma((19,)), out_s=dma((6,)),
        s1=dma((SIDE,)), v1=dma((SIDE,)), s2=dma((SIDE,)), v2=dma((SIDE,)),
        s3=dma((SIDE,)), v3=dma((SIDE,)), s4=dma((SIDE,)), v4=dma((SIDE,)),
        ks_s=dma((2,)), ks_v=dma, ka_s=dma((4,)), ka_v=dma((4,)), kb_s=dma((4,)), kb_v=dma((4,)),
        kr_s=dma, kr_v=dma, kc_s=dma((4,)), kc_v=dma((4,)), kf_s=dma((2,)), kf_v=dma,
        kh_s=dma((4,)), kh_v=dma((4,)), ki_s=dma((4,)), ki_v=dma((4,)),
        ga_s=dma, ga_v=dma, gb_s=dma((4,)), gb_v=dma((4,)), gf_s=dma((SIDE,)), gf_v=dma((SIDE,)),
    )
    shape = jax.ShapeDtypeStruct
    results = [shape(wide, BF)] * 3 + [shape((30, DG), F32)] * 2 + [shape((1, 15), F32)]
    held = pl.pallas_call(
        kernel,
        out_shape=results,
        in_specs=[hbm] * 10,
        out_specs=[hbm] * 6,
        scratch_shapes=scratch,
        compiler_params=pltpu.CompilerParams(
            collective_id=0, has_side_effects=True, vmem_limit_bytes=58 * 1024 * 1024
        ),
        cost_estimate=pl.CostEstimate(flops=4_000_000_000, bytes_accessed=6_000_000, transcendentals=600_000),
    )(
        inputs[0].T, cotangent[0].T, kernel_values.T, mix_in, mix_out,
        twiddle_self.transpose(1, 0, 2), twiddle_cross.transpose(1, 0, 2),
        norm_gain[None, :], up_weight, down_weight,
    )
    output, input_grad, kernel_grad, up_grad, down_grad, gain_grad = pl.pallas_call(
        settle,
        out_shape=results,
        in_specs=[hbm] * 6,
        out_specs=[hbm] * 6,
        scratch_shapes=[dma((6,))],
        compiler_params=pltpu.CompilerParams(vmem_limit_bytes=58 * 1024 * 1024),
        cost_estimate=pl.CostEstimate(flops=0, bytes_accessed=3_000_000, transcendentals=0),
    )(*held)
    return output.T[None], input_grad.T[None], kernel_grad.T, up_grad.T, down_grad.T, gain_grad[0]


def solution(mesh):
    in_specs = (
        P("dp", "seq", None),
        P("dp", "seq", None),
        P("seq", None),
        P("seq", None),
        P("seq", None),
        P(None, None, "seq"),
        P(None, None, "seq"),
        P(),
        P(),
        P(),
    )
    out_specs = (
        P("dp", "seq", None),
        P("dp", "seq", None),
        P("seq", None),
        P(None, "seq"),
        P(None, "seq"),
        P("seq"),
    )
    return jax.shard_map(local, mesh=mesh, in_specs=in_specs, out_specs=out_specs, check_vma=False)
```

time: 933 us -> 160 us (0.17); the launches traced: 916 us -> 160 us
  blocking collectives: 375 us -> 0 us
  waiting for transfers between devices: 309 us -> 0 us
  starting transfers between devices: 189 us -> 0 us
  Pallas kernels: 0 us -> 158 us
  other arithmetic: 16.1 us -> 0 us
  local copies, waits for them, and re-layouts: 13.6 us -> 1.27 us
  matrix products: 11 us -> 0 us
    ppermute x36 -> x0, waiting for transfers between devices: 309 us -> none  [swapped(): return lax.ppermute(value, axis, pairs)]
    unnamed x2 -> x0, blocking collectives: 267 us -> none
    ppermute x36 -> x0, starting transfers between devices: 177 us -> none  [swapped(): return lax.ppermute(value, axis, pairs)]
    pallas_call x0 -> x2, Pallas kernels: none -> 158 us  [the longest x1 110 us: local(): pl.pallas_call(kernel, out_shape=results, in_specs=[hbm] * 10, out_specs=...]
    psum x1 -> x0, blocking collectives: 108 us -> none  [local(): lax.psum(spectrum.astype(jnp.float32) * weighted_grad.astype(jnp.float32)...]
    convert_element_type x30 -> x0, other arithmetic: 13.1 us -> none  [the longest x27 11.5 us: rounded(): return lax.optimization_barrier(values.astype(jnp.bfloat16))]
    unnamed x8 -> x0, starting transfers between devices: 11.8 us -> none
    dot_general x10 -> x0, matrix products: 11 us -> none  [the longest x1 2.95 us: local(): jnp.einsum('tgf,tgj->jgf', activation, cot_blocks, preferred_element_type...]
  transfers between devices with their start and end apart: 44 -> 0, of which waited for: 26 -> 0; matrix products, arithmetic and copies ran while one was open for 19% -> 0% of each run, Pallas kernels for 0% -> 0%
where the time goes in v1:
time: 160 us
  Pallas kernels  158 us (99%)
    pallas_call x1, Pallas kernels, local(): pl.pallas_call(kernel, out_shape=results, in_specs=[hbm] * 10, out_specs=...  110 us
    pallas_call x1, Pallas kernels, local(): pl.pallas_call(settle, out_shape=results, in_specs=[hbm] * 6, out_specs=[...  47.8 us

profile of v1, /device:TPU:1, one launch (start us, length us, event | category | flops | bytes accessed | tf_op | source)
XLA Modules:
  0.0 160.2 jit_solution(3507530733323399673)
XLA Ops:
  0.6 0.0 copy-start
  0.6 0.7 copy-done
  1.3 0.6 broadcast_in_dim.9.gain_hbm
  1.9 110.5 %shard_map.145 = (bf16[960,256]{1,0:T(8,128)(2,1)}, bf16[960,256]{1,0:T(8,128)(2,1)}, bf16[960,256]{1,0:T(8,128)(2,1)}, f32[30,240]{1,0:T(8,128)}, f32[30,240]{1,0:T(8,128)}, /*index=5*/f32[1,15]{1,0:T(1,128)}) custom-call(bf16[960,256]{1,0:T(8,128)(2,1)} %bitcast.19, bf16[960,256]{1,0:T(8,128)(2,1)} %bitcast.20, bf16[960,256]{1,0:T(8,128)(2,1)} %bitcast.21, ...), custom_call_target="tpu_custom_call" | custom-call | flops 4000000000 | bytes 6000000 | tf_op jit(solution)/shard_map/pallas_call | solution.py:644
  112.4 47.8 %shard_map.146 = (bf16[960,256]{1,0:T(8,128)(2,1)}, bf16[960,256]{1,0:T(8,128)(2,1)}, bf16[960,256]{1,0:T(8,128)(2,1)}, f32[30,240]{1,0:T(8,128)}, f32[30,240]{1,0:T(8,128)}, /*index=5*/f32[1,15]{1,0:T(1,128)}) custom-call(bf16[960,256]{1,0:T(8,128)(2,1)} %get-tuple-element.18.refs_0_, bf16[960,256]{1,0:T(8,128)(2,1)} %get-tuple-element.19.refs_1_, ...), custom_call_target="tpu_custom_call" | custom-call | bytes 3000000 | tf_op jit(solution)/shard_map/pallas_call | solution.py:659
Async XLA Ops:
  0.6 0.7 copy-start

commit v2 on v1

--- a/solution.py
+++ b/solution.py
@@ -62,10 +62,10 @@
     for k, bit in bits:
         stride = 1 << bit
         if transposed:
-            scaled = [crosses[a][k] * values[a] for a in range(SIDE)]
-            values = [selfs[a][k] * values[a] + scaled[a ^ stride] for a in range(SIDE)]
+            scaled = [crosses(a, k) * values[a] for a in range(SIDE)]
+            values = [selfs(a, k) * values[a] + scaled[a ^ stride] for a in range(SIDE)]
         else:
-            values = [selfs[a][k] * values[a] + crosses[a][k] * values[a ^ stride] for a in range(SIDE)]
+            values = [selfs(a, k) * values[a] + crosses(a, k) * values[a ^ stride] for a in range(SIDE)]
     return values
 
 
@@ -75,9 +75,9 @@
     xv, kv, cotv, min_ref, mout_ref, ts_ref, tc_ref, gain_ref, up_ref, down_ref,
     outv, igv, kgv, ugv, dgv, gnv,
     eye, mint, moutt, twp, xg, cotg, cotn, upp, dnp, ww, acot, pa, act, pgr, hg, ng, ngr, hgr, acc, gaing, rowscale, wsum,
-    src1, a1, ks, kt, ff, sp, src2, m2, src3, a3, src4, m4,
+    src1, a1, ks, kt, ff, sp, src2, m2, src3, a3, src4, m4, src5, m5, twb,
     kgb, kra, kgh, krb, kgs, kgf, gg, r1a, h1, r1b, fin, rf,
-    in_s, out_s, s1, v1, s2, v2, s3, v3, s4, v4,
+    in_s, out_s, s1, v1, s2, v2, s3, v3, s4, v4, s5, v5,
     ks_s, ks_v, ka_s, ka_v, kb_s, kb_v, kr_s, kr_v, kc_s, kc_v, kf_s, kf_v, kh_s, kh_v, ki_s, ki_v,
     ga_s, ga_v, gb_s, gb_v, gf_s, gf_v,
 ):
@@ -145,11 +145,13 @@
 
     def store_grouped(ref, g, value):
         split = value.reshape(SIDE, 2, PIECE, 256)
-        ref[:, g, :, 0:256] = split[:, 0]
-        ref[:, 4 + g, :, 0:256] = split[:, 1]
+        for h in range(2):
+            ref[h, :, g] = split[:, 0, :, 128 * h : 128 * h + 128]
+            ref[h, :, 4 + g] = split[:, 1, :, 128 * h : 128 * h + 128]
 
     def load_grouped(ref, g):
-        return jnp.stack([ref[:, g, :, 0:256], ref[:, 4 + g, :, 0:256]], axis=1).reshape(256, 256)
+        halves = [jnp.stack([ref[h, :, g], ref[h, :, 4 + g]], axis=1).reshape(256, 128) for h in range(2)]
+        return jnp.concatenate(halves, axis=1)
 
     def slot(chip_at, core_at):
         return wrapped(2 * chip_at + core_at - y)
@@ -194,7 +196,9 @@
         copy.wait()
     for g in range(GROUPS):
         kv[g, pl.ds(DG, PIECE)] = twp[1, pl.ds(DG, PIECE)].astype(BF)
-        store_grouped(ks, g, dot_nt(eye[...], kv[g]).astype(BF))
+        split = dot_nt(eye[...], kv[g]).astype(BF).reshape(SIDE, 2, PIECE, 256)
+        ks[:, g] = split[:, 0]
+        ks[:, 4 + g] = split[:, 1]
     columns = dot_nt(eye[...], twp[0].astype(BF))
     for copy in x_here:
         copy.wait()
@@ -218,13 +222,18 @@
     def _():
         pltpu.make_async_copy(ks.at[z, yo], kt.at[y, z], ks_v).start()
 
-    first = (lambda tz, ty: src1.at[tz, ty], a1.at[z, y], s1, v1.at[z])
-    send_part(0, *first)
-    send_part(1, *first)
-    await_bytes(kt.at[yo], ks_v)
-    to_chips(kt, ka_s, ka_v)
-    send_part(2, *first)
-    send_part(3, *first)
+    def half_of(h, src, dst, ssem, rsem, at, group):
+        return (lambda tz, ty: src.at[h, tz, ty], dst.at[(h,) + at], ssem.at[h], rsem.at[h, group])
+
+    for h in (1, 0):
+        first = half_of(h, src1, a1, s1, v1, (z, y), z)
+        send_part(0, *first)
+        send_part(1, *first)
+        if h == 1:
+            await_bytes(kt.at[yo], ks_v)
+            to_chips(kt, ka_s, ka_v)
+        send_part(2, *first)
+        send_part(3, *first)
 
     for copy in rest_here:
         copy.wait()
@@ -255,17 +264,20 @@
         upp[g, DG:256] = jnp.zeros((256 - DG, 512), BF)
         dnp[g, DG:256] = jnp.zeros((256 - DG, 512), BF)
 
-    def twiddles(slab):
+    def spread_twiddles(which, p, q, slab):
         wide = slab.astype(F32)
-        return [wide[:, 112 + k : 113 + k] for k in range(6)], [wide[:, 120 + k : 121 + k] for k in range(6)]
-
-    def input_twiddles(shards):
-        pairs = [twiddles(a1[sz, sy, :, 128:256]) for sz, sy in shards]
-        return [p[0] for p in pairs], [p[1] for p in pairs]
-
-    def output_twiddles(shards):
-        pairs = [twiddles(kt[sy, sz, :, 128:256]) for sz, sy in shards]
-        return [p[0] for p in pairs], [p[1] for p in pairs]
+        for k in range(6):
+            twb[which, p, q, k] = jnp.broadcast_to(wide[:, 112 + k : 113 + k], (PIECE, 128))
+            twb[which, p, q, 6 + k] = jnp.broadcast_to(wide[:, 120 + k : 121 + k], (PIECE, 128))
+
+    def mixed(values, which, shards, bits, transposed):
+        def selfs(a, k):
+            return twb[which, shards[a][0], shards[a][1], k]
+
+        def crosses(a, k):
+            return twb[which, shards[a][0], shards[a][1], 6 + k]
+
+        return mix(values, selfs, crosses, bits, transposed)
 
     low_bits = ((0, 0), (1, 1), (2, 2))
     high_bits = ((3, 0), (4, 1), (5, 2))
@@ -278,45 +290,60 @@
     def column_of(sy):
         return [(a, sy) for a in range(SIDE)]
 
-    def forward_one(step):
-        sz = wrapped(z + step)
-        await_bytes(a1.at[sz], v1.at[sz])
-        shards = row_of(sz)
-        values = [a1[p, q].astype(F32) for p, q in shards]
-        values = mix(values, *input_twiddles(shards), low_bits, False)
-        for (p, q), value in zip(shards, values):
-            ff[p, q] = value
-
-    repeat(SIDE, forward_one)
+    def two_at_once(lines, read, which, bits, transposed, write):
+        def step(t):
+            groups = [lines(2 * t), lines(2 * t + 1)]
+            held = [[read(p, q) for p, q in shards] for shards in groups]
+            held = [mixed(values, which, shards, bits, transposed) for values, shards in zip(held, groups)]
+            for shards, values in zip(groups, held):
+                for (p, q), value in zip(shards, values):
+                    write(p, q, value)
+
+        repeat(SIDE // 2, step)
+
+    def store_wide(p, q, value):
+        ff[p, q] = value
+
+    def load_wide(p, q):
+        return ff[p, q]
+
     from_mate(kt, ka_v, kb_v)
 
-    def forward_two(sy):
-        shards = column_of(sy)
-        values = mix([ff[p, q] for p, q in shards], *input_twiddles(shards), high_bits, False)
-        for (p, q), value in zip(shards, values):
+    def spread_output_twiddles(sz):
+        for p, q in row_of(sz):
+            spread_twiddles(1, p, q, kt[q, p, :, 128:256])
+
+    repeat(SIDE, spread_output_twiddles)
+
+    for h in (1, 0):
+        lanes = slice(128 * h, 128 * h + 128)
+
+        def forward_one(step, h=h):
+            sz = wrapped(z + step)
+            await_bytes(a1.at[h, sz], v1.at[h, sz])
+            shards = row_of(sz)
+            if h == 1:
+                for p, q in shards:
+                    spread_twiddles(0, p, q, a1[1, p, q])
+            values = mixed([a1[h, p, q].astype(F32) for p, q in shards], 0, shards, low_bits, False)
+            for (p, q), value in zip(shards, values):
+                ff[p, q] = value
+
+        repeat(SIDE, forward_one)
+
+        def weigh(p, q, value, h=h, lanes=lanes):
             rounded = value.astype(BF)
-            sp[p, q] = rounded
-            ff[p, q] = rounded.astype(F32) * kt[q, p].astype(F32)
-
-    repeat(SIDE, forward_two)
-
-    def forward_three(sz):
-        shards = row_of(sz)
-        values = mix([ff[p, q] for p, q in shards], *output_twiddles(shards), low_bits, False)
-        for (p, q), value in zip(shards, values):
-            ff[p, q] = value
-
-    repeat(SIDE, forward_three)
-
-    def forward_four(sy):
-        shards = column_of(sy)
-        values = mix([ff[p, q] for p, q in shards], *output_twiddles(shards), high_bits, False)
-        for (p, q), value in zip(shards, values):
-            src2[p, q] = value.astype(BF)
-
-    repeat(SIDE, forward_four)
-    for part in range(4):
-        send_part(part, lambda tz, ty: src2.at[tz, ty], m2.at[z, y], s2, v2.at[z])
+            sp[h, p, q] = rounded
+            ff[p, q] = rounded.astype(F32) * kt[q, p, :, lanes].astype(F32)
+
+        def leave(p, q, value, h=h):
+            src2[h, p, q] = value.astype(BF)
+
+        two_at_once(column_of, load_wide, 0, high_bits, False, weigh)
+        two_at_once(row_of, load_wide, 1, low_bits, False, store_wide)
+        two_at_once(column_of, load_wide, 1, high_bits, False, leave)
+        for part in range(4):
+            send_part(part, *half_of(h, src2, m2, s2, v2, (z, y), z))
 
     for g in range(GROUPS):
         acot[g] = dot(cotg[g], dnp[g])
@@ -324,8 +351,9 @@
         spread = ones_where((channel == 4 * j + g) & (j < DG))
         ww[:, pl.ds(g * 512, 512)] = dot(spread, dnp[g]).astype(BF)
 
-    for sz in range(SIDE):
-        await_bytes(m2.at[sz], v2.at[sz])
+    for h in (1, 0):
+        for sz in range(SIDE):
+            await_bytes(m2.at[h, sz], v2.at[h, sz])
 
     lane_here = lax.broadcasted_iota(jnp.int32, (256, 256), 1) < DG
     squares = jnp.zeros((256, 1), F32)
@@ -344,7 +372,7 @@
         pa[...] = dot(ng[g], upp[g])
 
         def activate(tile, g=g):
-            rows = pl.ds(pl.multiple_of(tile * 32, 32), 32)
+            rows = pl.ds(pl.multiple_of(tile * 64, 64), 64)
             p = pa[rows]
             square = p * p
             tangent = jnp.tanh(p * (ROOT_HALF + (ROOT_HALF * CUBIC) * square))
@@ -354,7 +382,7 @@
             slope = half_more + 0.5 * p * (1.0 - tangent * tangent) * inner
             pgr[g, rows] = (acot[g, rows] * slope).astype(BF)
 
-        repeat(8, activate)
+        repeat(4, activate)
         ngr[g] = dot_nt(pgr[g], upp[g])
 
     means = jnp.zeros((256, 1), F32)
@@ -366,8 +394,9 @@
         gained = ngr[g] * gaing[g, 0:1]
         hgr[g] = (cotn[g].astype(F32) + scale_column * gained - hg[g].astype(F32) * means).astype(BF)
         store_grouped(src3, g, dot(moutt[...], hgr[g]).astype(BF))
-    for part in range(4):
-        send_part(part, lambda tz, ty: src3.at[tz, ty], a3.at[y, z], s3, v3.at[y])
+    for h in (1, 0):
+        for part in range(4):
+            send_part(part, *half_of(h, src3, a3, s3, v3, (y, z), y))
 
     row_here = (lax.broadcasted_iota(jnp.int32, (512, 256), 0) & 31) == 30
     for g in range(GROUPS):
@@ -382,12 +411,6 @@
 
     send(gg.at[1 - core], r1a, ga_s, ga_v, {"dp": mate})
 
-    acc[...] = dot_nt(ww[...], act[...])
-    for g in range(GROUPS):
-        rows = pl.ds(g * DG, DG)
-        outv[rows] = (acc[rows] + dot_nt(eye[0:DG], hg[g])).astype(BF)
-    pltpu.make_async_copy(outv, out_hbm, out_s.at[0]).start()
-
     await_bytes(r1a, ga_v)
 
     def pair_sum(step):
@@ -404,37 +427,41 @@
 
     repeat(4, spread_terms, 1)
 
-    def backward_one(step):
-        sy = wrapped(y + step)
-        await_bytes(a3.at[sy], v3.at[sy])
-        shards = column_of(sy)
-        values = [a3[q, p].astype(F32) for p, q in shards]
-        values = mix(values, *output_twiddles(shards), high_back, True)
-        for (p, q), value in zip(shards, values):
-            ff[p, q] = value
-
-    repeat(SIDE, backward_one)
-
-    def backward_two(sz):
-        shards = row_of(sz)
-        values = mix([ff[p, q] for p, q in shards], *output_twiddles(shards), low_back, True)
-        for (p, q), value in zip(shards, values):
+    others = [lax.rem(chip + step, 4) for step in (1, 2, 3)]
+
+    for h in (1, 0):
+        lanes = slice(128 * h, 128 * h + 128)
+
+        def backward_one(step, h=h):
+            sy = wrapped(y + step)
+            await_bytes(a3.at[h, sy], v3.at[h, sy])
+            shards = column_of(sy)
+            values = mixed([a3[h, q, p].astype(F32) for p, q in shards], 1, shards, high_back, True)
+            for (p, q), value in zip(shards, values):
+                ff[p, q] = value
+
+        repeat(SIDE, backward_one)
+
+        def weigh_back(p, q, value, h=h, lanes=lanes):
             wide = value.astype(BF).astype(F32)
             owner = wrapped(q + y)
-            kgb[lax.rem(owner, 2), lax.div(owner, 2), p] = (sp[p, q].astype(F32) * wide).astype(BF)
-            ff[p, q] = wide * kt[q, p].astype(F32)
-
-    repeat(SIDE, backward_two)
-
-    send(kgb.at[1 - core], kra, kr_s, kr_v, {"dp": mate})
-
-    def backward_three(sy):
-        shards = column_of(sy)
-        values = mix([ff[p, q] for p, q in shards], *input_twiddles(shards), high_back, True)
-        for (p, q), value in zip(shards, values):
-            ff[p, q] = value
-
-    repeat(SIDE, backward_three)
+            kgb[lax.rem(owner, 2), lax.div(owner, 2), p, :, lanes] = (sp[h, p, q].astype(F32) * wide).astype(BF)
+            ff[p, q] = wide * kt[q, p, :, lanes].astype(F32)
+
+        def leave_back(p, q, value, h=h):
+            src4[h, p, q] = value.astype(BF)
+
+        two_at_once(row_of, load_wide, 1, low_back, True, weigh_back)
+        if h == 0:
+            send(kgb.at[1 - core], kra, kr_s, kr_v, {"dp": mate})
+        two_at_once(column_of, load_wide, 0, high_back, True, store_wide)
+        two_at_once(row_of, load_wide, 0, low_back, True, leave_back)
+        last = half_of(h, src4, m4, s4, v4, (z, y), z)
+        send_part(0, *last)
+        send_part(1, *last)
+        if h == 1:
+            send_part(2, *last)
+            send_part(3, *last)
 
     await_bytes(kra, kr_v)
 
@@ -449,16 +476,8 @@
         send(kgh.at[other], krb.at[chip], kc_s.at[step], kc_v.at[step], {"dp": other * 2 + core})
 
     repeat(4, spread_kernel_terms, 1)
-
-    def backward_four(sz):
-        shards = row_of(sz)
-        values = mix([ff[p, q] for p, q in shards], *input_twiddles(shards), low_back, True)
-        for (p, q), value in zip(shards, values):
-            src4[p, q, :, 0:256] = value.astype(BF)
-
-    repeat(SIDE, backward_four)
-
-    others = [lax.rem(chip + step, 4) for step in (1, 2, 3)]
+    send_part(2, *last)
+    send_part(3, *last)
 
     def terms_here(step):
         await_bytes(r1b.at[lax.rem(chip + 4 - step, 4)], gb_v.at[step])
@@ -470,13 +489,9 @@
         four = h1[chip, part].astype(F32)
         for other in others:
             four = four + r1b[other, part].astype(F32)
-        src4[sz, :, :, 256:384] = four.astype(BF)
+        src5[sz] = four.astype(BF)
 
     repeat(SIDE, chip_sum)
-
-    last = (lambda tz, ty: src4.at[tz, ty], m4.at[z, y], s4, v4.at[z])
-    send_part(0, *last)
-    send_part(1, *last)
 
     def kernel_terms_here(step):
         await_bytes(krb.at[lax.rem(chip + 4 - step, 4)], kc_v.at[step])
@@ -505,36 +520,46 @@
     def _():
         pltpu.make_async_copy(kgs.at[z], kgf.at[y, z], kf_v).start()
 
-    send_part(2, *last)
-    send_part(3, *last)
+    for part in range(4):
+        send_part(part, lambda tz, ty: src5.at[tz, ty], m5.at[z, y], s5, v5.at[z])
+
+    acc[...] = dot_nt(ww[...], act[...])
+    for g in range(GROUPS):
+        rows = pl.ds(g * DG, DG)
+        outv[rows] = (acc[rows] + dot_nt(eye[0:DG], hg[g])).astype(BF)
+    pltpu.make_async_copy(outv, out_hbm, out_s.at[0]).start()
 
     await_bytes(kgf.at[yo], kf_v)
     to_chips(kgf, kh_s, kh_v)
+    for h in (1, 0):
+        for sz in range(SIDE):
+            await_bytes(m4.at[h, sz], v4.at[h, sz])
+    for g in range(GROUPS):
+        value = (hgr[g].astype(F32) + dot(mint[...], load_grouped(m4, g))).astype(BF)
+        igv[pl.ds(g * DG, DG)] = dot_nt(eye[0:DG], value).astype(BF)
+    pltpu.make_async_copy(igv, ig_hbm, out_s.at[2]).start()
+
     to_mate(kgf, kh_v, ki_s, ki_v)
+
+    shard_sum = jnp.zeros((PIECE, 128), F32)
+    for sz in range(SIDE):
+        await_bytes(m5.at[sz], v5.at[sz])
+        for sy in range(SIDE):
+            shard_sum = shard_sum + m5[sz, sy].astype(F32)
+    shard_sum = shard_sum * SCALE
+    fin[...] = shard_sum
+    rf[i] = shard_sum
+
+    def spread_grads(step):
+        send(fin, rf.at[i], gf_s.at[step], gf_v.at[step], {"dp": wrapped(i + step)})
+
+    repeat(SIDE, spread_grads, 1)
+
     from_mate(kgf, kh_v, ki_v)
     for g in range(GROUPS):
         held = jnp.stack([kgf[g], kgf[4 + g]], axis=1).reshape(256, 256)
         kgv[pl.ds(g * DG, DG)] = dot_nt(eye[0:DG], held).astype(BF)
     pltpu.make_async_copy(kgv, kg_hbm, out_s.at[1]).start()
-
-    shard_sum = jnp.zeros((PIECE, 128), F32)
-    for sz in range(SIDE):
-        await_bytes(m4.at[sz], v4.at[sz])
-        for sy in range(SIDE):
-            shard_sum = shard_sum + m4[sz, sy, :, 256:384].astype(F32)
-    shard_sum = shard_sum * SCALE
-    fin[...] = shard_sum
-    rf[i] = shard_sum
-
-    def spread_grads(step):
-        send(fin, rf.at[i], gf_s.at[step], gf_v.at[step], {"dp": wrapped(i + step)})
-
-    repeat(SIDE, spread_grads, 1)
-
-    for g in range(GROUPS):
-        value = (hgr[g].astype(F32) + dot(mint[...], load_grouped(m4, g))).astype(BF)
-        igv[pl.ds(g * DG, DG)] = dot_nt(eye[0:DG], value).astype(BF)
-    pltpu.make_async_copy(igv, ig_hbm, out_s.at[2]).start()
 
     def grads_here(step):
         await_bytes(rf.at[wrapped(i - step)], gf_v.at[step])
@@ -557,7 +582,9 @@
     pltpu.make_async_copy(gnv, gn_hbm, out_s.at[5]).start()
 
     for buffer, sem in ((src1, s1), (src2, s2), (src3, s3), (src4, s4)):
-        await_sent(buffer, sem)
+        for h in range(2):
+            await_sent(buffer.at[h], sem.at[h])
+    await_sent(src5, s5)
     await_bytes(ks.at[0, pl.ds(0, 7)], ks_s.at[1])
     await_bytes(kgs.at[pl.ds(0, 7)], kf_s.at[1])
 
@@ -591,11 +618,15 @@
 
 
 def settle(*refs):
-    held, there, sems = refs[:6], refs[6:12], refs[12]
-    copies = [pltpu.make_async_copy(held[index], there[index], sems.at[index]) for index in range(6)]
-    for copy in copies:
+    source, there, held, sems = refs[:6], refs[6:12], refs[12:18], refs[18]
+    loads = [pltpu.make_async_copy(source[index], held[index], sems.at[0, index]) for index in range(6)]
+    stores = [pltpu.make_async_copy(held[index], there[index], sems.at[1, index]) for index in range(6)]
+    for copy in loads:
         copy.start()
-    for copy in copies:
+    for load, store in zip(loads, stores):
+        load.wait()
+        store.start()
+    for copy in stores:
         copy.wait()
 
 
@@ -606,7 +637,9 @@
     dma = pltpu.SemaphoreType.DMA
     vmem = pltpu.VMEM
     exchange = vmem((SIDE, SIDE, PIECE, 256), BF)
-    longer = vmem((SIDE, SIDE, PIECE, 384), BF)
+    halves = vmem((2, SIDE, SIDE, PIECE, 128), BF)
+    part = vmem((SIDE, SIDE, PIECE, 128), BF)
+    both = dma((2, SIDE))
     grouped = vmem((GROUPS, 256, 256), BF)
     square = vmem((256, 256), BF)
     quarter = vmem((4, SIDE, PIECE, 256), BF)
@@ -625,15 +658,15 @@
         pgr=vmem((GROUPS, 256, 512), BF), hg=grouped, ng=grouped, ngr=vmem((GROUPS, 256, 256), F32),
         hgr=grouped, acc=vmem(wide, F32), gaing=vmem((GROUPS, 8, 256), F32), rowscale=vmem((256, 128), F32),
         wsum=vmem((2, 32, 256), F32),
-        src1=exchange, a1=exchange, ks=exchange, kt=exchange, ff=vmem((SIDE, SIDE, PIECE, 256), F32), sp=exchange,
-        src2=exchange, m2=exchange, src3=exchange, a3=exchange, src4=longer, m4=longer,
+        src1=halves, a1=halves, ks=exchange, kt=exchange, ff=vmem((SIDE, SIDE, PIECE, 128), F32), sp=halves,
+        src2=halves, m2=halves, src3=halves, a3=halves, src4=halves, m4=halves, src5=part, m5=part,
+        twb=vmem((2, SIDE, SIDE, 12, PIECE, 128), F32),
         kgb=vmem((2, 4, SIDE, PIECE, 256), BF), kra=quarter, kgh=quarter, krb=quarter,
         kgs=vmem((SIDE, PIECE, 256), BF), kgf=exchange,
         gg=vmem((2, 4, 64, PIECE, 128), BF), r1a=terms, h1=terms, r1b=terms,
         fin=vmem((PIECE, 128), F32), rf=vmem((SIDE, PIECE, 128), F32),
         in_s=dma((19,)), out_s=dma((6,)),
-        s1=dma((SIDE,)), v1=dma((SIDE,)), s2=dma((SIDE,)), v2=dma((SIDE,)),
-        s3=dma((SIDE,)), v3=dma((SIDE,)), s4=dma((SIDE,)), v4=dma((SIDE,)),
+        s1=both, v1=both, s2=both, v2=both, s3=both, v3=both, s4=both, v4=both, s5=dma((SIDE,)), v5=dma((SIDE,)),
         ks_s=dma((2,)), ks_v=dma, ka_s=dma((4,)), ka_v=dma((4,)), kb_s=dma((4,)), kb_v=dma((4,)),
         kr_s=dma, kr_v=dma, kc_s=dma((4,)), kc_v=dma((4,)), kf_s=dma((2,)), kf_v=dma,
         kh_s=dma((4,)), kh_v=dma((4,)), ki_s=dma((4,)), ki_v=dma((4,)),
@@ -661,7 +694,7 @@
         out_shape=results,
         in_specs=[hbm] * 6,
         out_specs=[hbm] * 6,
-        scratch_shapes=[dma((6,))],
+        scratch_shapes=[vmem(result.shape, result.dtype) for result in results] + [dma((2, 6))],
         compiler_params=pltpu.CompilerParams(vmem_limit_bytes=58 * 1024 * 1024),
         cost_estimate=pl.CostEstimate(flops=0, bytes_accessed=3_000_000, transcendentals=0),
     )(*held)

time: 160 us -> 107 us (0.67)
  Pallas kernels: 158 us -> 105 us
    pallas_call x1, Pallas kernels: 47.8 us -> 2.25 us  [local(): pl.pallas_call(settle, out_shape=results, in_specs=[hbm] * 6, out_specs=[...]
    pallas_call x1, Pallas kernels: 110 us -> 103 us  [local(): pl.pallas_call(kernel, out_shape=results, in_specs=[hbm] * 10, out_specs=...]
where the time goes in v2:
time: 107 us
  Pallas kernels  105 us (98%)
  local copies, waits for them, and re-layouts  1.27 us (1%)
    pallas_call x1, Pallas kernels, local(): pl.pallas_call(kernel, out_shape=results, in_specs=[hbm] * 10, out_specs=...  103 us
    pallas_call x1, Pallas kernels, local(): pl.pallas_call(settle, out_shape=results, in_specs=[hbm] * 6, out_specs=[...  2.25 us

profile of v2, /device:TPU:1, one launch (start us, length us, event | category | flops | bytes accessed | tf_op | source)
XLA Modules:
  0.0 107.1 jit_solution(16501027929571635533)
XLA Ops:
  0.6 0.0 copy-start
  0.6 0.7 copy-done
  1.3 0.6 broadcast_in_dim.9.gain_hbm
  1.9 102.8 %shard_map.145 = (bf16[960,256]{1,0:T(8,128)(2,1)}, bf16[960,256]{1,0:T(8,128)(2,1)}, bf16[960,256]{1,0:T(8,128)(2,1)}, f32[30,240]{1,0:T(8,128)}, f32[30,240]{1,0:T(8,128)}, /*index=5*/f32[1,15]{1,0:T(1,128)}) custom-call(bf16[960,256]{1,0:T(8,128)(2,1)} %bitcast.19, bf16[960,256]{1,0:T(8,128)(2,1)} %bitcast.20, bf16[960,256]{1,0:T(8,128)(2,1)} %bitcast.21, ...), custom_call_target="tpu_custom_call" | custom-call | flops 4000000000 | bytes 6000000 | tf_op jit(solution)/shard_map/pallas_call | solution.py:677
  104.7 2.2 %shard_map.146 = (bf16[960,256]{1,0:T(8,128)(2,1)}, bf16[960,256]{1,0:T(8,128)(2,1)}, bf16[960,256]{1,0:T(8,128)(2,1)}, f32[30,240]{1,0:T(8,128)}, f32[30,240]{1,0:T(8,128)}, /*index=5*/f32[1,15]{1,0:T(1,128)}) custom-call(bf16[960,256]{1,0:T(8,128)(2,1)} %get-tuple-element.18.refs_0_, bf16[960,256]{1,0:T(8,128)(2,1)} %get-tuple-element.19.refs_1_, ...), custom_call_target="tpu_custom_call" | custom-call | bytes 3000000 | tf_op jit(solution)/shard_map/pallas_call | solution.py:692
Async XLA Ops:
  0.6 0.7 copy-start

commit v3 on v2

--- a/solution.py
+++ b/solution.py
@@ -75,9 +75,9 @@
     xv, kv, cotv, min_ref, mout_ref, ts_ref, tc_ref, gain_ref, up_ref, down_ref,
     outv, igv, kgv, ugv, dgv, gnv,
     eye, mint, moutt, twp, xg, cotg, cotn, upp, dnp, ww, acot, pa, act, pgr, hg, ng, ngr, hgr, acc, gaing, rowscale, wsum,
-    src1, a1, ks, kt, ff, sp, src2, m2, src3, a3, src4, m4, src5, m5, twb,
+    src1, a1, ks, kt, ff, sp, src2, m2, src3, a3, src4, m4, twb, pa1, pa2, pa3, pb1, pb2, pb3, pc,
     kgb, kra, kgh, krb, kgs, kgf, gg, r1a, h1, r1b, fin, rf,
-    in_s, out_s, s1, v1, s2, v2, s3, v3, s4, v4, s5, v5,
+    in_s, out_s, s1, v1, s2, v2, s3, v3, s4, v4, pa_s, pa_v, pb_s, pb_v, pc_s, pc_v, pd_s,
     ks_s, ks_v, ka_s, ka_v, kb_s, kb_v, kr_s, kr_v, kc_s, kc_v, kf_s, kf_v, kh_s, kh_v, ki_s, ki_v,
     ga_s, ga_v, gb_s, gb_v, gf_s, gf_v,
 ):
@@ -124,34 +124,44 @@
         ).start()
 
     def send_part(part, src, dst, ssem, rsem):
+        offsets = ((3, 5, 1, 7), (2, 6, 4, 0))[part]
+
         def one(dz, dy):
             tz, ty = wrapped(z + dz), wrapped(y + dy)
             send(src(tz, ty), dst, ssem.at[dz], rsem, {"seq": tz * SIDE + ty})
 
-        if part == 0:
+        def pair(t):
+            for dy in (3 - t, 5 + t):
+                for dz in offsets:
+                    one(dz, dy)
+
+        repeat(3, pair)
+        for dy in (4, 0):
+            for dz in offsets:
+                if (dz, dy) != (0, 0):
+                    one(dz, dy)
+        if part == 1:
             pltpu.make_async_copy(src(z, y), dst, rsem).start()
-            one(4, 0)
-
-        def pair(t):
-            one(part, lax.rem(5 * t, SIDE))
-            one((4, 7, 6, 5)[part], lax.rem(5 * t, SIDE))
-
-        repeat(SIDE, pair, 1 if part == 0 else 0)
 
     def await_sent(buffer, ssem):
         await_bytes(buffer.at[0, pl.ds(0, 7)], ssem.at[0])
         for dz in range(1, SIDE):
             await_bytes(buffer.at[0], ssem.at[dz])
 
-    def store_grouped(ref, g, value):
-        split = value.reshape(SIDE, 2, PIECE, 256)
-        for h in range(2):
-            ref[h, :, g] = split[:, 0, :, 128 * h : 128 * h + 128]
-            ref[h, :, 4 + g] = split[:, 1, :, 128 * h : 128 * h + 128]
-
-    def load_grouped(ref, g):
-        halves = [jnp.stack([ref[h, :, g], ref[h, :, 4 + g]], axis=1).reshape(256, 128) for h in range(2)]
-        return jnp.concatenate(halves, axis=1)
+    def store_half(ref, h, pair, value):
+        for side in range(2):
+            split = value[:, 128 * side : 128 * side + 128].reshape(SIDE, 2, PIECE, 128)
+            ref[h, :, 2 * pair + side] = split[:, 0]
+            ref[h, :, 4 + 2 * pair + side] = split[:, 1]
+
+    def load_half(ref, h, pair):
+        groups = (2 * pair, 2 * pair + 1)
+        return jnp.concatenate(
+            [jnp.stack([ref[h, :, g], ref[h, :, 4 + g]], axis=1).reshape(256, 128) for g in groups], axis=1
+        )
+
+    def half_lanes(ref, h, pair):
+        return jnp.concatenate([ref[2 * pair + side, :, 128 * h : 128 * h + 128] for side in range(2)], axis=1)
 
     def slot(chip_at, core_at):
         return wrapped(2 * chip_at + core_at - y)
@@ -199,13 +209,21 @@
         split = dot_nt(eye[...], kv[g]).astype(BF).reshape(SIDE, 2, PIECE, 256)
         ks[:, g] = split[:, 0]
         ks[:, 4 + g] = split[:, 1]
-    columns = dot_nt(eye[...], twp[0].astype(BF))
+    columns = dot_nt(eye[...], twp[0].astype(BF))[:, 128:256]
     for copy in x_here:
         copy.wait()
     for g in range(GROUPS):
         xv[g, pl.ds(DG, PIECE)] = jnp.zeros((PIECE, 256), BF)
-        store_grouped(src1, g, (dot_nt(min_ref[...], xv[g]) + columns).astype(BF))
-
+
+    def premix(h):
+        for pair in range(2):
+            rows = jnp.concatenate([xv[2 * pair + side, 128 * h : 128 * h + 128] for side in range(2)], axis=0)
+            value = dot_nt(min_ref[...], rows)
+            if h == 1:
+                value = value + jnp.concatenate([columns, columns], axis=1)
+            store_half(src1, h, pair, value.astype(BF))
+
+    premix(1)
     pl.semaphore_wait(barrier, 70)
 
     def share_kernel(dz):
@@ -227,13 +245,13 @@
 
     for h in (1, 0):
         first = half_of(h, src1, a1, s1, v1, (z, y), z)
+        if h == 0:
+            premix(0)
         send_part(0, *first)
-        send_part(1, *first)
         if h == 1:
             await_bytes(kt.at[yo], ks_v)
             to_chips(kt, ka_s, ka_v)
-        send_part(2, *first)
-        send_part(3, *first)
+        send_part(1, *first)
 
     for copy in rest_here:
         copy.wait()
@@ -342,7 +360,7 @@
         two_at_once(column_of, load_wide, 0, high_bits, False, weigh)
         two_at_once(row_of, load_wide, 1, low_bits, False, store_wide)
         two_at_once(column_of, load_wide, 1, high_bits, False, leave)
-        for part in range(4):
+        for part in range(2):
             send_part(part, *half_of(h, src2, m2, s2, v2, (z, y), z))
 
     for g in range(GROUPS):
@@ -351,18 +369,20 @@
         spread = ones_where((channel == 4 * j + g) & (j < DG))
         ww[:, pl.ds(g * 512, 512)] = dot(spread, dnp[g]).astype(BF)
 
+    lane_here = (lax.broadcasted_iota(jnp.int32, (256, 256), 1) & 127) < DG - 128
+    squares = jnp.zeros((256, 1), F32)
     for h in (1, 0):
         for sz in range(SIDE):
             await_bytes(m2.at[h, sz], v2.at[h, sz])
-
-    lane_here = lax.broadcasted_iota(jnp.int32, (256, 256), 1) < DG
-    squares = jnp.zeros((256, 1), F32)
-    for g in range(GROUPS):
-        value = xg[g].astype(F32) + dot(mout_ref[...], load_grouped(m2, g))
-        value = jnp.where(lane_here, value, 0.0).astype(BF)
-        hg[g] = value
-        wide = value.astype(F32)
-        squares = squares + jnp.sum(wide * wide, axis=1, keepdims=True)
+        for pair in range(2):
+            value = half_lanes(xg, h, pair).astype(F32) + dot(mout_ref[...], load_half(m2, h, pair))
+            if h == 1:
+                value = jnp.where(lane_here, value, 0.0)
+            value = value.astype(BF)
+            for side in range(2):
+                hg[2 * pair + side, :, 128 * h : 128 * h + 128] = value[:, 128 * side : 128 * side + 128]
+            wide = value.astype(F32)
+            squares = squares + jnp.sum(wide * wide, axis=1, keepdims=True)
     scale_column = lax.rsqrt(squares * (1.0 / D) + 1e-06)
     rowscale[...] = jnp.broadcast_to(scale_column, (256, 128))
 
@@ -390,12 +410,15 @@
         means = means + jnp.sum(ngr[g] * gaing[g, 0:1] * hg[g].astype(F32), axis=1, keepdims=True)
     scale_column = rowscale[:, 0:1]
     means = means * (1.0 / D) * scale_column * scale_column * scale_column
-    for g in range(GROUPS):
-        gained = ngr[g] * gaing[g, 0:1]
-        hgr[g] = (cotn[g].astype(F32) + scale_column * gained - hg[g].astype(F32) * means).astype(BF)
-        store_grouped(src3, g, dot(moutt[...], hgr[g]).astype(BF))
     for h in (1, 0):
-        for part in range(4):
+        lanes = slice(128 * h, 128 * h + 128)
+        for pair in range(2):
+            for g in (2 * pair, 2 * pair + 1):
+                gained = ngr[g, :, lanes] * gaing[g, 0:1, lanes]
+                wide = hg[g, :, lanes].astype(F32)
+                hgr[g, :, lanes] = (cotn[g, :, lanes].astype(F32) + scale_column * gained - wide * means).astype(BF)
+            store_half(src3, h, pair, dot(moutt[...], half_lanes(hgr, h, pair)).astype(BF))
+        for part in range(2):
             send_part(part, *half_of(h, src3, a3, s3, v3, (y, z), y))
 
     row_here = (lax.broadcasted_iota(jnp.int32, (512, 256), 0) & 31) == 30
@@ -458,10 +481,8 @@
         two_at_once(row_of, load_wide, 0, low_back, True, leave_back)
         last = half_of(h, src4, m4, s4, v4, (z, y), z)
         send_part(0, *last)
-        send_part(1, *last)
         if h == 1:
-            send_part(2, *last)
-            send_part(3, *last)
+            send_part(1, *last)
 
     await_bytes(kra, kr_v)
 
@@ -476,22 +497,41 @@
         send(kgh.at[other], krb.at[chip], kc_s.at[step], kc_v.at[step], {"dp": other * 2 + core})
 
     repeat(4, spread_kernel_terms, 1)
-    send_part(2, *last)
-    send_part(3, *last)
 
     def terms_here(step):
         await_bytes(r1b.at[lax.rem(chip + 4 - step, 4)], gb_v.at[step])
 
     repeat(4, terms_here, 1)
 
-    def chip_sum(sz):
-        part = pl.ds(pl.multiple_of(sz * 8, 8), 8)
-        four = h1[chip, part].astype(F32)
-        for other in others:
-            four = four + r1b[other, part].astype(F32)
-        src5[sz] = four.astype(BF)
-
-    repeat(SIDE, chip_sum)
+    def chip_sum(t):
+        for odd in range(2):
+            sz = 2 * t + odd
+            part = pl.ds(pl.multiple_of(sz * 8, 8), 8)
+            four = h1[chip, part].astype(F32)
+            for other in others:
+                four = four + r1b[other, part].astype(F32)
+            four = four.astype(BF)
+            for q in range(SIDE):
+                if (odd + q) % 2 == 0:
+                    pa1[q, t] = four[q]
+                else:
+                    pb1[sz, q // 2] = four[q]
+
+    repeat(SIDE // 2, chip_sum)
+
+    def along_y(step):
+        ty = wrapped(y + step)
+        send(pa1.at[ty], pa2.at[y], pa_s.at[step], pa_v.at[step], {"seq": z * SIDE + ty})
+
+    def along_z(step):
+        tz = wrapped(z + step)
+        send(pb1.at[tz], pb2.at[z], pb_s.at[step], pb_v.at[step], {"seq": tz * SIDE + y})
+
+    def first_step(step):
+        along_y(step)
+        along_z(step)
+
+    repeat(SIDE, first_step, 1)
 
     def kernel_terms_here(step):
         await_bytes(krb.at[lax.rem(chip + 4 - step, 4)], kc_v.at[step])
@@ -520,8 +560,7 @@
     def _():
         pltpu.make_async_copy(kgs.at[z], kgf.at[y, z], kf_v).start()
 
-    for part in range(4):
-        send_part(part, lambda tz, ty: src5.at[tz, ty], m5.at[z, y], s5, v5.at[z])
+    send_part(1, *last)
 
     acc[...] = dot_nt(ww[...], act[...])
     for g in range(GROUPS):
@@ -529,23 +568,56 @@
         outv[rows] = (acc[rows] + dot_nt(eye[0:DG], hg[g])).astype(BF)
     pltpu.make_async_copy(outv, out_hbm, out_s.at[0]).start()
 
+    def first_here(step):
+        await_bytes(pa2.at[wrapped(y - step)], pa_v.at[step])
+        await_bytes(pb2.at[wrapped(z - step)], pb_v.at[step])
+
+    repeat(SIDE, first_here, 1)
+    sum_y, sum_z = pa1[y].astype(F32), pb1[z].astype(F32)
+    for step in range(1, SIDE):
+        sum_y = sum_y + pa2[wrapped(y + step)].astype(F32)
+        sum_z = sum_z + pb2[wrapped(z + step)].astype(F32)
+    pa3[...] = sum_y.astype(BF)
+    pb3[...] = sum_z.astype(BF)
+    odd = lax.rem(z + y, 2)
+
+    def second_z(m):
+        return 2 * m + lax.rem(y, 2)
+
+    def second_y(m):
+        return 2 * m + 1 - lax.rem(z, 2)
+
+    for m in range(4):
+
+        @pl.when(second_z(m) != z)
+        def _(m=m):
+            send(pa3.at[m], pc.at[z], pc_s.at[m], pc_v.at[z], {"seq": second_z(m) * SIDE + y})
+
+        @pl.when(second_y(m) != y)
+        def _(m=m):
+            send(pb3.at[m], pc.at[y], pd_s.at[m], pc_v.at[y], {"seq": z * SIDE + second_y(m)})
+
+    @pl.when(odd == 0)
+    def _():
+        pc[z] = pa3[lax.div(z, 2)]
+
+    @pl.when(odd == 1)
+    def _():
+        pc[y] = pb3[lax.div(y, 2)]
+
     await_bytes(kgf.at[yo], kf_v)
     to_chips(kgf, kh_s, kh_v)
-    for h in (1, 0):
-        for sz in range(SIDE):
-            await_bytes(m4.at[h, sz], v4.at[h, sz])
-    for g in range(GROUPS):
-        value = (hgr[g].astype(F32) + dot(mint[...], load_grouped(m4, g))).astype(BF)
-        igv[pl.ds(g * DG, DG)] = dot_nt(eye[0:DG], value).astype(BF)
-    pltpu.make_async_copy(igv, ig_hbm, out_s.at[2]).start()
-
-    to_mate(kgf, kh_v, ki_s, ki_v)
-
-    shard_sum = jnp.zeros((PIECE, 128), F32)
-    for sz in range(SIDE):
-        await_bytes(m5.at[sz], v5.at[sz])
-        for sy in range(SIDE):
-            shard_sum = shard_sum + m5[sz, sy].astype(F32)
+
+    own = z + odd * (y - z)
+
+    def second_here(step):
+        at = wrapped(own + step)
+        await_bytes(pc.at[at], pc_v.at[at])
+
+    repeat(SIDE, second_here, 1)
+    shard_sum = pc[0].astype(F32)
+    for at in range(1, SIDE):
+        shard_sum = shard_sum + pc[at].astype(F32)
     shard_sum = shard_sum * SCALE
     fin[...] = shard_sum
     rf[i] = shard_sum
@@ -554,6 +626,20 @@
         send(fin, rf.at[i], gf_s.at[step], gf_v.at[step], {"dp": wrapped(i + step)})
 
     repeat(SIDE, spread_grads, 1)
+    to_mate(kgf, kh_v, ki_s, ki_v)
+
+    for h in (1, 0):
+        lanes = slice(128 * h, 128 * h + 128)
+        for sz in range(SIDE):
+            await_bytes(m4.at[h, sz], v4.at[h, sz])
+        for pair in range(2):
+            value = half_lanes(hgr, h, pair).astype(F32) + dot(mint[...], load_half(m4, h, pair))
+            value = dot_nt(eye[...], value.astype(BF)).astype(BF)
+            for side in range(2):
+                start = (2 * pair + side) * DG + 128 * h
+                rows = DG - 128 if h == 1 else 128
+                igv[pl.ds(start, rows)] = value[128 * side : 128 * side + rows]
+    pltpu.make_async_copy(igv, ig_hbm, out_s.at[2]).start()
 
     from_mate(kgf, kh_v, ki_v)
     for g in range(GROUPS):
@@ -584,7 +670,16 @@
     for buffer, sem in ((src1, s1), (src2, s2), (src3, s3), (src4, s4)):
         for h in range(2):
             await_sent(buffer.at[h], sem.at[h])
-    await_sent(src5, s5)
+    for m in range(4):
+
+        @pl.when(second_z(m) != z)
+        def _(m=m):
+            await_bytes(pa3.at[m], pc_s.at[m])
+
+        @pl.when(second_y(m) != y)
+        def _(m=m):
+            await_bytes(pb3.at[m], pd_s.at[m])
+
     await_bytes(ks.at[0, pl.ds(0, 7)], ks_s.at[1])
     await_bytes(kgs.at[pl.ds(0, 7)], kf_s.at[1])
 
@@ -610,6 +705,8 @@
 
     def grads_left(step):
         await_bytes(fin, gf_s.at[step])
+        await_bytes(pa1.at[0], pa_s.at[step])
+        await_bytes(pb1.at[0], pb_s.at[step])
 
     repeat(SIDE, grads_left, 1)
     outs = ((outv, out_hbm), (kgv, kg_hbm), (igv, ig_hbm), (ugv, ug_hbm), (dgv, dg_hbm), (gnv, gn_hbm))
@@ -638,7 +735,7 @@
     vmem = pltpu.VMEM
     exchange = vmem((SIDE, SIDE, PIECE, 256), BF)
     halves = vmem((2, SIDE, SIDE, PIECE, 128), BF)
-    part = vmem((SIDE, SIDE, PIECE, 128), BF)
+    part = vmem((SIDE, 4, PIECE, 128), BF)
     both = dma((2, SIDE))
     grouped = vmem((GROUPS, 256, 256), BF)
     square = vmem((256, 256), BF)
@@ -659,14 +756,18 @@
         hgr=grouped, acc=vmem(wide, F32), gaing=vmem((GROUPS, 8, 256), F32), rowscale=vmem((256, 128), F32),
         wsum=vmem((2, 32, 256), F32),
         src1=halves, a1=halves, ks=exchange, kt=exchange, ff=vmem((SIDE, SIDE, PIECE, 128), F32), sp=halves,
-        src2=halves, m2=halves, src3=halves, a3=halves, src4=halves, m4=halves, src5=part, m5=part,
+        src2=halves, m2=halves, src3=halves, a3=halves, src4=halves, m4=halves,
+        pa1=part, pa2=part, pa3=vmem((4, PIECE, 128), BF), pb1=part, pb2=part, pb3=vmem((4, PIECE, 128), BF),
+        pc=vmem((SIDE, PIECE, 128), BF),
         twb=vmem((2, SIDE, SIDE, 12, PIECE, 128), F32),
         kgb=vmem((2, 4, SIDE, PIECE, 256), BF), kra=quarter, kgh=quarter, krb=quarter,
         kgs=vmem((SIDE, PIECE, 256), BF), kgf=exchange,
         gg=vmem((2, 4, 64, PIECE, 128), BF), r1a=terms, h1=terms, r1b=terms,
         fin=vmem((PIECE, 128), F32), rf=vmem((SIDE, PIECE, 128), F32),
         in_s=dma((19,)), out_s=dma((6,)),
-        s1=both, v1=both, s2=both, v2=both, s3=both, v3=both, s4=both, v4=both, s5=dma((SIDE,)), v5=dma((SIDE,)),
+        s1=both, v1=both, s2=both, v2=both, s3=both, v3=both, s4=both, v4=both,
+        pa_s=dma((SIDE,)), pa_v=dma((SIDE,)), pb_s=dma((SIDE,)), pb_v=dma((SIDE,)),
+        pc_s=dma((4,)), pc_v=dma((SIDE,)), pd_s=dma((4,)),
         ks_s=dma((2,)), ks_v=dma, ka_s=dma((4,)), ka_v=dma((4,)), kb_s=dma((4,)), kb_v=dma((4,)),
         kr_s=dma, kr_v=dma, kc_s=dma((4,)), kc_v=dma((4,)), kf_s=dma((2,)), kf_v=dma,
         kh_s=dma((4,)), kh_v=dma((4,)), ki_s=dma((4,)), ki_v=dma((4,)),

time: 107 us -> 104 us (0.972)
  Pallas kernels: 105 us -> 102 us
    pallas_call x1, Pallas kernels: 103 us -> 99.4 us  [local(): pl.pallas_call(kernel, out_shape=results, in_specs=[hbm] * 10, out_specs=...]
where the time goes in v3:
time: 104 us
  Pallas kernels  102 us (98%)
  local copies, waits for them, and re-layouts  1.27 us (1%)
    pallas_call x1, Pallas kernels, local(): pl.pallas_call(kernel, out_shape=results, in_specs=[hbm] * 10, out_specs=...  99.4 us
    pallas_call x1, Pallas kernels, local(): pl.pallas_call(settle, out_shape=results, in_specs=[hbm] * 6, out_specs=[...  2.25 us

profile of v3, /device:TPU:1, one launch (start us, length us, event | category | flops | bytes accessed | tf_op | source)
XLA Modules:
  0.0 103.7 jit_solution(3680446675036107442)
XLA Ops:
  0.6 0.0 copy-start
  0.6 0.7 copy-done
  1.3 0.6 broadcast_in_dim.9.gain_hbm
  1.9 99.4 %shard_map.145 = (bf16[960,256]{1,0:T(8,128)(2,1)}, bf16[960,256]{1,0:T(8,128)(2,1)}, bf16[960,256]{1,0:T(8,128)(2,1)}, f32[30,240]{1,0:T(8,128)}, f32[30,240]{1,0:T(8,128)}, /*index=5*/f32[1,15]{1,0:T(1,128)}) custom-call(bf16[960,256]{1,0:T(8,128)(2,1)} %bitcast.19, bf16[960,256]{1,0:T(8,128)(2,1)} %bitcast.20, bf16[960,256]{1,0:T(8,128)(2,1)} %bitcast.21, ...), custom_call_target="tpu_custom_call" | custom-call | flops 4000000000 | bytes 6000000 | tf_op jit(solution)/shard_map/pallas_call | solution.py:778
  101.3 2.2 %shard_map.146 = (bf16[960,256]{1,0:T(8,128)(2,1)}, bf16[960,256]{1,0:T(8,128)(2,1)}, bf16[960,256]{1,0:T(8,128)(2,1)}, f32[30,240]{1,0:T(8,128)}, f32[30,240]{1,0:T(8,128)}, /*index=5*/f32[1,15]{1,0:T(1,128)}) custom-call(bf16[960,256]{1,0:T(8,128)(2,1)} %get-tuple-element.18.refs_0_, bf16[960,256]{1,0:T(8,128)(2,1)} %get-tuple-element.19.refs_1_, ...), custom_call_target="tpu_custom_call" | custom-call | bytes 3000000 | tf_op jit(solution)/shard_map/pallas_call | solution.py:793
Async XLA Ops:
  0.6 0.7 copy-start

commit v4 on v3

--- a/solution.py
+++ b/solution.py
@@ -104,16 +104,18 @@
     chip, core = lax.div(i, 2), lax.rem(i, 2)
     mate = i + 1 - 2 * core
     yo = wrapped(i - y)
+    tz_at = [wrapped(z + step) for step in range(SIDE)]
+    ty_at = [wrapped(y + step) for step in range(SIDE)]
 
     barrier = pltpu.get_barrier_semaphore()
 
     def greet_seq(step):
         pl.semaphore_signal(
-            barrier, inc=1, device_id={"seq": lax.rem(me + step, 64)}, device_id_type=MESH
+            barrier, inc=1, device_id=(i, lax.rem(me + step, 64)), device_id_type=MESH
         )
 
     def greet_dp(step):
-        pl.semaphore_signal(barrier, inc=1, device_id={"dp": wrapped(i + step)}, device_id_type=MESH)
+        pl.semaphore_signal(barrier, inc=1, device_id=(wrapped(i + step), me), device_id_type=MESH)
 
     repeat(64, greet_seq, 1)
     repeat(8, greet_dp, 1)
@@ -126,20 +128,21 @@
     def send_part(part, src, dst, ssem, rsem):
         offsets = ((3, 5, 1, 7), (2, 6, 4, 0))[part]
 
-        def one(dz, dy):
-            tz, ty = wrapped(z + dz), wrapped(y + dy)
-            send(src(tz, ty), dst, ssem.at[dz], rsem, {"seq": tz * SIDE + ty})
+        def one(dz, ty):
+            tz = tz_at[dz]
+            send(src(tz, ty), dst, ssem.at[dz], rsem, (i, tz * SIDE + ty))
 
         def pair(t):
             for dy in (3 - t, 5 + t):
+                ty = wrapped(y + dy)
                 for dz in offsets:
-                    one(dz, dy)
+                    one(dz, ty)
 
         repeat(3, pair)
         for dy in (4, 0):
             for dz in offsets:
                 if (dz, dy) != (0, 0):
-                    one(dz, dy)
+                    one(dz, ty_at[dy])
         if part == 1:
             pltpu.make_async_copy(src(z, y), dst, rsem).start()
 
@@ -167,12 +170,12 @@
         return wrapped(2 * chip_at + core_at - y)
 
     def to_chips(buffer, ssem, rsem):
-        send(buffer.at[yo], buffer.at[yo], ssem.at[0], rsem.at[0], {"dp": mate})
+        send(buffer.at[yo], buffer.at[yo], ssem.at[0], rsem.at[0], (mate, me))
 
         def step_to(step):
             send(
                 buffer.at[yo], buffer.at[yo], ssem.at[step], rsem.at[step],
-                {"dp": 2 * lax.rem(chip + step, 4) + core},
+                (2 * lax.rem(chip + step, 4) + core, me),
             )
 
         repeat(4, step_to, 1)
@@ -181,7 +184,7 @@
         def step_to(step):
             held = buffer.at[slot(lax.rem(chip + 4 - step, 4), core)]
             await_bytes(held, rsem.at[step])
-            send(held, held, ssem2.at[step], rsem2.at[step], {"dp": mate})
+            send(held, held, ssem2.at[step], rsem2.at[step], (mate, me))
 
         repeat(4, step_to, 1)
 
@@ -228,13 +231,13 @@
 
     def share_kernel(dz):
         tz = wrapped(z + dz)
-        send(ks.at[tz, yo], kt.at[y, z], ks_s.at[1], ks_v, {"seq": tz * SIDE + yo})
+        send(ks.at[tz, yo], kt.at[y, z], ks_s.at[1], ks_v, (i, tz * SIDE + yo))
 
     repeat(SIDE, share_kernel, 1)
 
     @pl.when(yo != y)
     def _():
-        send(ks.at[z, yo], kt.at[y, z], ks_s.at[0], ks_v, {"seq": z * SIDE + yo})
+        send(ks.at[z, yo], kt.at[y, z], ks_s.at[0], ks_v, (i, z * SIDE + yo))
 
     @pl.when(yo == y)
     def _():
@@ -246,6 +249,7 @@
     for h in (1, 0):
         first = half_of(h, src1, a1, s1, v1, (z, y), z)
         if h == 0:
+            to_mate(kt, ka_v, kb_s, kb_v)
             premix(0)
         send_part(0, *first)
         if h == 1:
@@ -253,35 +257,6 @@
             to_chips(kt, ka_s, ka_v)
         send_part(1, *first)
 
-    for copy in rest_here:
-        copy.wait()
-    for g in range(GROUPS):
-        xg[g] = dot_nt(eye[...], xv[g]).astype(BF)
-        cotv[g, pl.ds(DG, PIECE)] = jnp.zeros((PIECE, 256), BF)
-    mint[...] = dot_nt(eye[...], min_ref[...]).astype(BF)
-    moutt[...] = dot_nt(eye[...], mout_ref[...]).astype(BF)
-    for g in range(GROUPS):
-        cotn[g] = dot_nt(eye[...], cotv[g]).astype(BF)
-        picked = jnp.zeros((256, 256), F32)
-        for part in range(GROUPS):
-            j, lane = iotas((256, 256))
-            picked = picked + dot(ones_where((part * DG + lane == 4 * j + g) & (lane < DG)), cotv[part])
-        cotg[g] = dot_nt(eye[...], picked.astype(BF)).astype(BF)
-        low, high = GAIN_WINDOWS[g]
-        channel, lane = iotas((high - low, 256))
-        gain_rows = jnp.broadcast_to(gain_ref[:, low:high].astype(F32), (PIECE, high - low)).astype(BF)
-        gaing[g] = dot(gain_rows, ones_where((channel + low == g * DG + lane) & (lane < DG)))[0:8]
-    to_mate(kt, ka_v, kb_s, kb_v)
-    for g in range(GROUPS):
-        low, high = HIDDEN_WINDOWS[g]
-        column, hidden_unit = iotas((high - low, 512))
-        chosen = (column + low == g * FFG + hidden_unit - 2 * (hidden_unit >> 5)) & ((hidden_unit & 31) < 30)
-        chooser = ones_where(chosen)
-        upp[g, 0:DG] = dot(up_ref[:, low:high], chooser).astype(BF)
-        dnp[g, 0:DG] = dot(down_ref[:, low:high], chooser).astype(BF)
-        upp[g, DG:256] = jnp.zeros((256 - DG, 512), BF)
-        dnp[g, DG:256] = jnp.zeros((256 - DG, 512), BF)
-
     def spread_twiddles(which, p, q, slab):
         wide = slab.astype(F32)
         for k in range(6):
@@ -308,14 +283,16 @@
     def column_of(sy):
         return [(a, sy) for a in range(SIDE)]
 
+    def work(groups, read, which, bits, transposed, write):
+        held = [[read(p, q) for p, q in shards] for shards in groups]
+        held = [mixed(values, which, shards, bits, transposed) for values, shards in zip(held, groups)]
+        for shards, values in zip(groups, held):
+            for (p, q), value in zip(shards, values):
+                write(p, q, value)
+
     def two_at_once(lines, read, which, bits, transposed, write):
         def step(t):
-            groups = [lines(2 * t), lines(2 * t + 1)]
-            held = [[read(p, q) for p, q in shards] for shards in groups]
-            held = [mixed(values, which, shards, bits, transposed) for values, shards in zip(held, groups)]
-            for shards, values in zip(groups, held):
-                for (p, q), value in zip(shards, values):
-                    write(p, q, value)
+            work([lines(2 * t), lines(2 * t + 1)], read, which, bits, transposed, write)
 
         repeat(SIDE // 2, step)
 
@@ -359,9 +336,49 @@
 
         two_at_once(column_of, load_wide, 0, high_bits, False, weigh)
         two_at_once(row_of, load_wide, 1, low_bits, False, store_wide)
-        two_at_once(column_of, load_wide, 1, high_bits, False, leave)
-        for part in range(2):
-            send_part(part, *half_of(h, src2, m2, s2, v2, (z, y), z))
+
+        def forward_four(dys, h=h):
+            columns = [wrapped(y + dy) for dy in dys]
+            work([column_of(sy) for sy in columns], load_wide, 1, high_bits, False, leave)
+            for dy, sy in zip(dys, columns):
+                for dz, sz in enumerate(tz_at):
+                    if dz == 0 and isinstance(dy, int) and dy == 0:
+                        pltpu.make_async_copy(src2.at[h, z, y], m2.at[h, z, y], v2.at[h, z]).start()
+                    else:
+                        send(src2.at[h, sz, sy], m2.at[h, z, y], s2.at[h, dz], v2.at[h, z], (i, sz * SIDE + sy))
+
+        forward_four((0, 4))
+        repeat(4, lambda t: forward_four((t, SIDE - t)), 1)
+        if h == 1:
+            for copy in rest_here:
+                copy.wait()
+            for g in range(GROUPS):
+                xg[g] = dot_nt(eye[...], xv[g]).astype(BF)
+                cotv[g, pl.ds(DG, PIECE)] = jnp.zeros((PIECE, 256), BF)
+            mint[...] = dot_nt(eye[...], min_ref[...]).astype(BF)
+            moutt[...] = dot_nt(eye[...], mout_ref[...]).astype(BF)
+            for g in range(GROUPS):
+                cotn[g] = dot_nt(eye[...], cotv[g]).astype(BF)
+                picked = jnp.zeros((256, 256), F32)
+                for part in range(GROUPS):
+                    j, lane = iotas((256, 256))
+                    picked = picked + dot(ones_where((part * DG + lane == 4 * j + g) & (lane < DG)), cotv[part])
+                cotg[g] = dot_nt(eye[...], picked.astype(BF)).astype(BF)
+                low, high = GAIN_WINDOWS[g]
+                channel, lane = iotas((high - low, 256))
+                gain_rows = jnp.broadcast_to(gain_ref[:, low:high].astype(F32), (PIECE, high - low)).astype(BF)
+                gaing[g] = dot(gain_rows, ones_where((channel + low == g * DG + lane) & (lane < DG)))[0:8]
+
+
+    for g in range(GROUPS):
+        low, high = HIDDEN_WINDOWS[g]
+        column, hidden_unit = iotas((high - low, 512))
+        chosen = (column + low == g * FFG + hidden_unit - 2 * (hidden_unit >> 5)) & ((hidden_unit & 31) < 30)
+        chooser = ones_where(chosen)
+        upp[g, 0:DG] = dot(up_ref[:, low:high], chooser).astype(BF)
+        dnp[g, 0:DG] = dot(down_ref[:, low:high], chooser).astype(BF)
+        upp[g, DG:256] = jnp.zeros((256 - DG, 512), BF)
+        dnp[g, DG:256] = jnp.zeros((256 - DG, 512), BF)
 
     for g in range(GROUPS):
         acot[g] = dot(cotg[g], dnp[g])
@@ -392,7 +409,7 @@
         pa[...] = dot(ng[g], upp[g])
 
         def activate(tile, g=g):
-            rows = pl.ds(pl.multiple_of(tile * 64, 64), 64)
+            rows = pl.ds(pl.multiple_of(tile * 32, 32), 32)
             p = pa[rows]
             square = p * p
             tangent = jnp.tanh(p * (ROOT_HALF + (ROOT_HALF * CUBIC) * square))
@@ -402,7 +419,7 @@
             slope = half_more + 0.5 * p * (1.0 - tangent * tangent) * inner
             pgr[g, rows] = (acot[g, rows] * slope).astype(BF)
 
-        repeat(4, activate)
+        repeat(8, activate)
         ngr[g] = dot_nt(pgr[g], upp[g])
 
     means = jnp.zeros((256, 1), F32)
@@ -432,23 +449,7 @@
                 for side in range(2):
                     gg[side, 2 * kind + half, pl.ds(g * 16, 16)] = split[:, half, :, side * 128 : side * 128 + 128]
 
-    send(gg.at[1 - core], r1a, ga_s, ga_v, {"dp": mate})
-
-    await_bytes(r1a, ga_v)
-
-    def pair_sum(step):
-        for slab in range(4):
-            part = pl.ds(pl.multiple_of(step * 8, 8), 8)
-            both = gg[core, slab, part].astype(F32) + r1a[slab, part].astype(F32)
-            h1[slab, part] = both.astype(BF)
-
-    repeat(8, pair_sum)
-
-    def spread_terms(step):
-        other = lax.rem(chip + step, 4)
-        send(h1.at[other], r1b.at[chip], gb_s.at[step], gb_v.at[step], {"dp": other * 2 + core})
-
-    repeat(4, spread_terms, 1)
+    send(gg.at[1 - core], r1a, ga_s, ga_v, (mate, me))
 
     others = [lax.rem(chip + step, 4) for step in (1, 2, 3)]
 
@@ -476,13 +477,48 @@
 
         two_at_once(row_of, load_wide, 1, low_back, True, weigh_back)
         if h == 0:
-            send(kgb.at[1 - core], kra, kr_s, kr_v, {"dp": mate})
+            send(kgb.at[1 - core], kra, kr_s, kr_v, (mate, me))
         two_at_once(column_of, load_wide, 0, high_back, True, store_wide)
-        two_at_once(row_of, load_wide, 0, low_back, True, leave_back)
-        last = half_of(h, src4, m4, s4, v4, (z, y), z)
-        send_part(0, *last)
+
+        def send_rows(dzs, h=h):
+            for dz in dzs:
+                sz = wrapped(z + dz)
+                for dy, sy in enumerate(ty_at):
+                    if dy == 0 and isinstance(dz, int) and dz == 0:
+                        pltpu.make_async_copy(src4.at[h, z, y], m4.at[h, z, y], v4.at[h, z]).start()
+                    else:
+                        send(src4.at[h, sz, sy], m4.at[h, z, y], s4.at[h, dz], v4.at[h, z], (i, sz * SIDE + sy))
+
+        def backward_four(dzs):
+            work([row_of(wrapped(z + dz)) for dz in dzs], load_wide, 0, low_back, True, leave_back)
+
+        def backward_four_sent(dzs):
+            backward_four(dzs)
+            send_rows(dzs)
+
         if h == 1:
-            send_part(1, *last)
+            await_bytes(r1a, ga_v)
+
+            def pair_sum(step):
+                for slab in range(4):
+                    part = pl.ds(pl.multiple_of(step * 8, 8), 8)
+                    both = gg[core, slab, part].astype(F32) + r1a[slab, part].astype(F32)
+                    h1[slab, part] = both.astype(BF)
+
+            repeat(8, pair_sum)
+
+            def spread_terms(step):
+                other = lax.rem(chip + step, 4)
+                send(h1.at[other], r1b.at[chip], gb_s.at[step], gb_v.at[step], (other * 2 + core, me))
+
+            repeat(4, spread_terms, 1)
+
+        backward_four_sent((0, 4))
+        if h == 1:
+            repeat(4, lambda t: backward_four_sent((t, SIDE - t)), 1)
+        else:
+            repeat(2, lambda t: backward_four_sent((t, SIDE - t)), 1)
+            repeat(4, lambda t: backward_four((t, SIDE - t)), 2)
 
     await_bytes(kra, kr_v)
 
@@ -494,7 +530,7 @@
 
     def spread_kernel_terms(step):
         other = lax.rem(chip + step, 4)
-        send(kgh.at[other], krb.at[chip], kc_s.at[step], kc_v.at[step], {"dp": other * 2 + core})
+        send(kgh.at[other], krb.at[chip], kc_s.at[step], kc_v.at[step], (other * 2 + core, me))
 
     repeat(4, spread_kernel_terms, 1)
 
@@ -521,11 +557,11 @@
 
     def along_y(step):
         ty = wrapped(y + step)
-        send(pa1.at[ty], pa2.at[y], pa_s.at[step], pa_v.at[step], {"seq": z * SIDE + ty})
+        send(pa1.at[ty], pa2.at[y], pa_s.at[step], pa_v.at[step], (i, z * SIDE + ty))
 
     def along_z(step):
         tz = wrapped(z + step)
-        send(pb1.at[tz], pb2.at[z], pb_s.at[step], pb_v.at[step], {"seq": tz * SIDE + y})
+        send(pb1.at[tz], pb2.at[z], pb_s.at[step], pb_v.at[step], (i, tz * SIDE + y))
 
     def first_step(step):
         along_y(step)
@@ -548,19 +584,19 @@
 
     def return_kernel(dz):
         tz = wrapped(z + dz)
-        send(kgs.at[tz], kgf.at[y, z], kf_s.at[1], kf_v, {"seq": tz * SIDE + yo})
+        send(kgs.at[tz], kgf.at[y, z], kf_s.at[1], kf_v, (i, tz * SIDE + yo))
 
     repeat(SIDE, return_kernel, 1)
 
     @pl.when(yo != y)
     def _():
-        send(kgs.at[z], kgf.at[y, z], kf_s.at[0], kf_v, {"seq": z * SIDE + yo})
+        send(kgs.at[z], kgf.at[y, z], kf_s.at[0], kf_v, (i, z * SIDE + yo))
 
     @pl.when(yo == y)
     def _():
         pltpu.make_async_copy(kgs.at[z], kgf.at[y, z], kf_v).start()
 
-    send_part(1, *last)
+    repeat(4, lambda t: send_rows((t, SIDE - t)), 2)
 
     acc[...] = dot_nt(ww[...], act[...])
     for g in range(GROUPS):
@@ -591,11 +627,11 @@
 
         @pl.when(second_z(m) != z)
         def _(m=m):
-            send(pa3.at[m], pc.at[z], pc_s.at[m], pc_v.at[z], {"seq": second_z(m) * SIDE + y})
+            send(pa3.at[m], pc.at[z], pc_s.at[m], pc_v.at[z], (i, second_z(m) * SIDE + y))
 
         @pl.when(second_y(m) != y)
         def _(m=m):
-            send(pb3.at[m], pc.at[y], pd_s.at[m], pc_v.at[y], {"seq": z * SIDE + second_y(m)})
+            send(pb3.at[m], pc.at[y], pd_s.at[m], pc_v.at[y], (i, z * SIDE + second_y(m)))
 
     @pl.when(odd == 0)
     def _():
@@ -623,7 +659,7 @@
     rf[i] = shard_sum
 
     def spread_grads(step):
-        send(fin, rf.at[i], gf_s.at[step], gf_v.at[step], {"dp": wrapped(i + step)})
+        send(fin, rf.at[i], gf_s.at[step], gf_v.at[step], (wrapped(i + step), me))
 
     repeat(SIDE, spread_grads, 1)
     to_mate(kgf, kh_v, ki_s, ki_v)

time: 104 us -> 109 us (1.048)
  Pallas kernels: 102 us -> 106 us
    pallas_call x1, Pallas kernels: 99.4 us -> 103 us  [local(): pl.pallas_call(kernel, out_shape=results, in_specs=[hbm] * 10, out_specs=...]
where the time goes in v4:
time: 109 us; the launch traced here: 108 us
  Pallas kernels  106 us (97%)
  local copies, waits for them, and re-layouts  1.27 us (1%)
    pallas_call x1, Pallas kernels, local(): pl.pallas_call(kernel, out_shape=results, in_specs=[hbm] * 10, out_specs=...  103 us
    pallas_call x1, Pallas kernels, local(): pl.pallas_call(settle, out_shape=results, in_specs=[hbm] * 6, out_specs=[...  2.25 us

profile of v4, /device:TPU:1, one launch (start us, length us, event | category | flops | bytes accessed | tf_op | source)
XLA Modules:
  0.0 107.8 jit_solution(16418684911578420772)
XLA Ops:
  0.6 0.0 copy-start
  0.6 0.7 copy-done
  1.3 0.6 broadcast_in_dim.9.gain_hbm
  1.9 103.5 %shard_map.145 = (bf16[960,256]{1,0:T(8,128)(2,1)}, bf16[960,256]{1,0:T(8,128)(2,1)}, bf16[960,256]{1,0:T(8,128)(2,1)}, f32[30,240]{1,0:T(8,128)}, f32[30,240]{1,0:T(8,128)}, /*index=5*/f32[1,15]{1,0:T(1,128)}) custom-call(bf16[960,256]{1,0:T(8,128)(2,1)} %bitcast.19, bf16[960,256]{1,0:T(8,128)(2,1)} %bitcast.20, bf16[960,256]{1,0:T(8,128)(2,1)} %bitcast.21, ...), custom_call_target="tpu_custom_call" | custom-call | flops 4000000000 | bytes 6000000 | tf_op jit(solution)/shard_map/pallas_call | solution.py:814
  105.4 2.2 %shard_map.146 = (bf16[960,256]{1,0:T(8,128)(2,1)}, bf16[960,256]{1,0:T(8,128)(2,1)}, bf16[960,256]{1,0:T(8,128)(2,1)}, f32[30,240]{1,0:T(8,128)}, f32[30,240]{1,0:T(8,128)}, /*index=5*/f32[1,15]{1,0:T(1,128)}) custom-call(bf16[960,256]{1,0:T(8,128)(2,1)} %get-tuple-element.18.refs_0_, bf16[960,256]{1,0:T(8,128)(2,1)} %get-tuple-element.19.refs_1_, ...), custom_call_target="tpu_custom_call" | custom-call | bytes 3000000 | tf_op jit(solution)/shard_map/pallas_call | solution.py:829
Async XLA Ops:
  0.6 0.7 copy-start

commit v5 on v4

--- a/solution.py
+++ b/solution.py
@@ -249,12 +249,13 @@
     for h in (1, 0):
         first = half_of(h, src1, a1, s1, v1, (z, y), z)
         if h == 0:
-            to_mate(kt, ka_v, kb_s, kb_v)
             premix(0)
         send_part(0, *first)
         if h == 1:
             await_bytes(kt.at[yo], ks_v)
             to_chips(kt, ka_s, ka_v)
+        else:
+            to_mate(kt, ka_v, kb_s, kb_v)
         send_part(1, *first)
 
     def spread_twiddles(which, p, q, slab):
@@ -283,16 +284,14 @@
     def column_of(sy):
         return [(a, sy) for a in range(SIDE)]
 
-    def work(groups, read, which, bits, transposed, write):
-        held = [[read(p, q) for p, q in shards] for shards in groups]
-        held = [mixed(values, which, shards, bits, transposed) for values, shards in zip(held, groups)]
-        for shards, values in zip(groups, held):
-            for (p, q), value in zip(shards, values):
-                write(p, q, value)
-
     def two_at_once(lines, read, which, bits, transposed, write):
         def step(t):
-            work([lines(2 * t), lines(2 * t + 1)], read, which, bits, transposed, write)
+            groups = [lines(2 * t), lines(2 * t + 1)]
+            held = [[read(p, q) for p, q in shards] for shards in groups]
+            held = [mixed(values, which, shards, bits, transposed) for values, shards in zip(held, groups)]
+            for shards, values in zip(groups, held):
+                for (p, q), value in zip(shards, values):
+                    write(p, q, value)
 
         repeat(SIDE // 2, step)
 
@@ -336,19 +335,9 @@
 
         two_at_once(column_of, load_wide, 0, high_bits, False, weigh)
         two_at_once(row_of, load_wide, 1, low_bits, False, store_wide)
-
-        def forward_four(dys, h=h):
-            columns = [wrapped(y + dy) for dy in dys]
-            work([column_of(sy) for sy in columns], load_wide, 1, high_bits, False, leave)
-            for dy, sy in zip(dys, columns):
-                for dz, sz in enumerate(tz_at):
-                    if dz == 0 and isinstance(dy, int) and dy == 0:
-                        pltpu.make_async_copy(src2.at[h, z, y], m2.at[h, z, y], v2.at[h, z]).start()
-                    else:
-                        send(src2.at[h, sz, sy], m2.at[h, z, y], s2.at[h, dz], v2.at[h, z], (i, sz * SIDE + sy))
-
-        forward_four((0, 4))
-        repeat(4, lambda t: forward_four((t, SIDE - t)), 1)
+        two_at_once(column_of, load_wide, 1, high_bits, False, leave)
+        for part in range(2):
+            send_part(part, *half_of(h, src2, m2, s2, v2, (z, y), z))
         if h == 1:
             for copy in rest_here:
                 copy.wait()
@@ -409,7 +398,7 @@
         pa[...] = dot(ng[g], upp[g])
 
         def activate(tile, g=g):
-            rows = pl.ds(pl.multiple_of(tile * 32, 32), 32)
+            rows = pl.ds(pl.multiple_of(tile * 64, 64), 64)
             p = pa[rows]
             square = p * p
             tangent = jnp.tanh(p * (ROOT_HALF + (ROOT_HALF * CUBIC) * square))
@@ -419,7 +408,7 @@
             slope = half_more + 0.5 * p * (1.0 - tangent * tangent) * inner
             pgr[g, rows] = (acot[g, rows] * slope).astype(BF)
 
-        repeat(8, activate)
+        repeat(4, activate)
         ngr[g] = dot_nt(pgr[g], upp[g])
 
     means = jnp.zeros((256, 1), F32)
@@ -427,6 +416,22 @@
         means = means + jnp.sum(ngr[g] * gaing[g, 0:1] * hg[g].astype(F32), axis=1, keepdims=True)
     scale_column = rowscale[:, 0:1]
     means = means * (1.0 / D) * scale_column * scale_column * scale_column
+    def split_terms(kind, g, term):
+        split = term.astype(BF).reshape(16, 2, PIECE, 256)
+        for half in range(2):
+            for side in range(2):
+                gg[side, 2 * kind + half, pl.ds(g * 16, 16)] = split[:, half, :, side * 128 : side * 128 + 128]
+
+    def weight_terms():
+        row_here = (lax.broadcasted_iota(jnp.int32, (512, 256), 0) & 31) == 30
+        for g in range(GROUPS):
+            split_terms(1, g, dot_tn(act[:, pl.ds(g * 512, 512)], cotg[g]))
+        send(gg.at[1 - core, pl.ds(2, 2)], r1a.at[pl.ds(2, 2)], ga_s.at[1], ga_v.at[1], (mate, me))
+        for g in range(GROUPS):
+            gain_term = jnp.sum(ngr[g] * hg[g].astype(F32) * rowscale[:, 0:1], axis=0, keepdims=True)
+            split_terms(0, g, jnp.where(row_here, gain_term, dot_tn(pgr[g], ng[g])))
+        send(gg.at[1 - core, pl.ds(0, 2)], r1a.at[pl.ds(0, 2)], ga_s.at[0], ga_v.at[0], (mate, me))
+
     for h in (1, 0):
         lanes = slice(128 * h, 128 * h + 128)
         for pair in range(2):
@@ -437,19 +442,25 @@
             store_half(src3, h, pair, dot(moutt[...], half_lanes(hgr, h, pair)).astype(BF))
         for part in range(2):
             send_part(part, *half_of(h, src3, a3, s3, v3, (y, z), y))
-
-    row_here = (lax.broadcasted_iota(jnp.int32, (512, 256), 0) & 31) == 30
-    for g in range(GROUPS):
-        gain_term = jnp.sum(ngr[g] * hg[g].astype(F32) * rowscale[:, 0:1], axis=0, keepdims=True)
-        up_term = jnp.where(row_here, gain_term, dot_tn(pgr[g], ng[g]))
-        down_term = dot_tn(act[:, pl.ds(g * 512, 512)], cotg[g])
-        for kind, term in ((0, up_term), (1, down_term)):
-            split = term.astype(BF).reshape(16, 2, PIECE, 256)
-            for half in range(2):
-                for side in range(2):
-                    gg[side, 2 * kind + half, pl.ds(g * 16, 16)] = split[:, half, :, side * 128 : side * 128 + 128]
-
-    send(gg.at[1 - core], r1a, ga_s, ga_v, (mate, me))
+        if h == 1:
+            weight_terms()
+
+    for kind in (1, 0):
+        await_bytes(r1a.at[pl.ds(2 * kind, 2)], ga_v.at[kind])
+
+    def pair_sum(step):
+        for slab in range(4):
+            part = pl.ds(pl.multiple_of(step * 8, 8), 8)
+            both = gg[core, slab, part].astype(F32) + r1a[slab, part].astype(F32)
+            h1[slab, part] = both.astype(BF)
+
+    repeat(8, pair_sum)
+
+    def spread_terms(step):
+        other = lax.rem(chip + step, 4)
+        send(h1.at[other], r1b.at[chip], gb_s.at[step], gb_v.at[step], (other * 2 + core, me))
+
+    repeat(4, spread_terms, 1)
 
     others = [lax.rem(chip + step, 4) for step in (1, 2, 3)]
 
@@ -479,46 +490,11 @@
         if h == 0:
             send(kgb.at[1 - core], kra, kr_s, kr_v, (mate, me))
         two_at_once(column_of, load_wide, 0, high_back, True, store_wide)
-
-        def send_rows(dzs, h=h):
-            for dz in dzs:
-                sz = wrapped(z + dz)
-                for dy, sy in enumerate(ty_at):
-                    if dy == 0 and isinstance(dz, int) and dz == 0:
-                        pltpu.make_async_copy(src4.at[h, z, y], m4.at[h, z, y], v4.at[h, z]).start()
-                    else:
-                        send(src4.at[h, sz, sy], m4.at[h, z, y], s4.at[h, dz], v4.at[h, z], (i, sz * SIDE + sy))
-
-        def backward_four(dzs):
-            work([row_of(wrapped(z + dz)) for dz in dzs], load_wide, 0, low_back, True, leave_back)
-
-        def backward_four_sent(dzs):
-            backward_four(dzs)
-            send_rows(dzs)
-
+        two_at_once(row_of, load_wide, 0, low_back, True, leave_back)
+        last = half_of(h, src4, m4, s4, v4, (z, y), z)
+        send_part(0, *last)
         if h == 1:
-            await_bytes(r1a, ga_v)
-
-            def pair_sum(step):
-                for slab in range(4):
-                    part = pl.ds(pl.multiple_of(step * 8, 8), 8)
-                    both = gg[core, slab, part].astype(F32) + r1a[slab, part].astype(F32)
-                    h1[slab, part] = both.astype(BF)
-
-            repeat(8, pair_sum)
-
-            def spread_terms(step):
-                other = lax.rem(chip + step, 4)
-                send(h1.at[other], r1b.at[chip], gb_s.at[step], gb_v.at[step], (other * 2 + core, me))
-
-            repeat(4, spread_terms, 1)
-
-        backward_four_sent((0, 4))
-        if h == 1:
-            repeat(4, lambda t: backward_four_sent((t, SIDE - t)), 1)
-        else:
-            repeat(2, lambda t: backward_four_sent((t, SIDE - t)), 1)
-            repeat(4, lambda t: backward_four((t, SIDE - t)), 2)
+            send_part(1, *last)
 
     await_bytes(kra, kr_v)
 
@@ -533,6 +509,35 @@
         send(kgh.at[other], krb.at[chip], kc_s.at[step], kc_v.at[step], (other * 2 + core, me))
 
     repeat(4, spread_kernel_terms, 1)
+
+    def kernel_terms_here(step):
+        await_bytes(krb.at[lax.rem(chip + 4 - step, 4)], kc_v.at[step])
+
+    repeat(4, kernel_terms_here, 1)
+
+    def kernel_sum(sz):
+        four = kgh[chip, sz].astype(F32)
+        for other in others:
+            four = four + krb[other, sz].astype(F32)
+        kgs[sz] = four.astype(BF)
+
+    repeat(SIDE, kernel_sum)
+
+    def return_kernel(dz):
+        tz = wrapped(z + dz)
+        send(kgs.at[tz], kgf.at[y, z], kf_s.at[1], kf_v, (i, tz * SIDE + yo))
+
+    repeat(SIDE, return_kernel, 1)
+
+    @pl.when(yo != y)
+    def _():
+        send(kgs.at[z], kgf.at[y, z], kf_s.at[0], kf_v, (i, z * SIDE + yo))
+
+    @pl.when(yo == y)
+    def _():
+        pltpu.make_async_copy(kgs.at[z], kgf.at[y, z], kf_v).start()
+
+    send_part(1, *last)
 
     def terms_here(step):
         await_bytes(r1b.at[lax.rem(chip + 4 - step, 4)], gb_v.at[step])
@@ -568,35 +573,6 @@
         along_z(step)
 
     repeat(SIDE, first_step, 1)
-
-    def kernel_terms_here(step):
-        await_bytes(krb.at[lax.rem(chip + 4 - step, 4)], kc_v.at[step])
-
-    repeat(4, kernel_terms_here, 1)
-
-    def kernel_sum(sz):
-        four = kgh[chip, sz].astype(F32)
-        for other in others:
-            four = four + krb[other, sz].astype(F32)
-        kgs[sz] = four.astype(BF)
-
-    repeat(SIDE, kernel_sum)
-
-    def return_kernel(dz):
-        tz = wrapped(z + dz)
-        send(kgs.at[tz], kgf.at[y, z], kf_s.at[1], kf_v, (i, tz * SIDE + yo))
-
-    repeat(SIDE, return_kernel, 1)
-
-    @pl.when(yo != y)
-    def _():
-        send(kgs.at[z], kgf.at[y, z], kf_s.at[0], kf_v, (i, z * SIDE + yo))
-
-    @pl.when(yo == y)
-    def _():
-        pltpu.make_async_copy(kgs.at[z], kgf.at[y, z], kf_v).start()
-
-    repeat(4, lambda t: send_rows((t, SIDE - t)), 2)
 
     acc[...] = dot_nt(ww[...], act[...])
     for g in range(GROUPS):
@@ -726,7 +702,8 @@
 
     await_bytes(kt.at[0], ka_s.at[0])
     await_bytes(kgf.at[0], kh_s.at[0])
-    await_bytes(r1a, ga_s)
+    for kind in range(2):
+        await_bytes(r1a.at[pl.ds(0, 2)], ga_s.at[kind])
     await_bytes(kra, kr_s)
 
     def chips_left(step):
@@ -807,7 +784,7 @@
         ks_s=dma((2,)), ks_v=dma, ka_s=dma((4,)), ka_v=dma((4,)), kb_s=dma((4,)), kb_v=dma((4,)),
         kr_s=dma, kr_v=dma, kc_s=dma((4,)), kc_v=dma((4,)), kf_s=dma((2,)), kf_v=dma,
         kh_s=dma((4,)), kh_v=dma((4,)), ki_s=dma((4,)), ki_v=dma((4,)),
-        ga_s=dma, ga_v=dma, gb_s=dma((4,)), gb_v=dma((4,)), gf_s=dma((SIDE,)), gf_v=dma((SIDE,)),
+        ga_s=dma((2,)), ga_v=dma((2,)), gb_s=dma((4,)), gb_v=dma((4,)), gf_s=dma((SIDE,)), gf_v=dma((SIDE,)),
     )
     shape = jax.ShapeDtypeStruct
     results = [shape(wide, BF)] * 3 + [shape((30, DG), F32)] * 2 + [shape((1, 15), F32)]

time: 109 us -> 109 us (level)
  no operation moved by 1% of the time
where the time goes in v5:
time: 109 us; the launch traced here: 108 us
  Pallas kernels  106 us (97%)
  local copies, waits for them, and re-layouts  1.27 us (1%)
    pallas_call x1, Pallas kernels, local(): pl.pallas_call(kernel, out_shape=results, in_specs=[hbm] * 10, out_specs=...  104 us
    pallas_call x1, Pallas kernels, local(): pl.pallas_call(settle, out_shape=results, in_specs=[hbm] * 6, out_specs=[...  2.25 us

profile of v5, /device:TPU:1, one launch (start us, length us, event | category | flops | bytes accessed | tf_op | source)
XLA Modules:
  0.0 108.3 jit_solution(1605218949800574236)
XLA Ops:
  0.6 0.0 copy-start
  0.6 0.7 copy-done
  1.3 0.6 broadcast_in_dim.9.gain_hbm
  1.9 104.0 %shard_map.145 = (bf16[960,256]{1,0:T(8,128)(2,1)}, bf16[960,256]{1,0:T(8,128)(2,1)}, bf16[960,256]{1,0:T(8,128)(2,1)}, f32[30,240]{1,0:T(8,128)}, f32[30,240]{1,0:T(8,128)}, /*index=5*/f32[1,15]{1,0:T(1,128)}) custom-call(bf16[960,256]{1,0:T(8,128)(2,1)} %bitcast.19, bf16[960,256]{1,0:T(8,128)(2,1)} %bitcast.20, bf16[960,256]{1,0:T(8,128)(2,1)} %bitcast.21, ...), custom_call_target="tpu_custom_call" | custom-call | flops 4000000000 | bytes 6000000 | tf_op jit(solution)/shard_map/pallas_call | solution.py:791
  105.9 2.2 %shard_map.146 = (bf16[960,256]{1,0:T(8,128)(2,1)}, bf16[960,256]{1,0:T(8,128)(2,1)}, bf16[960,256]{1,0:T(8,128)(2,1)}, f32[30,240]{1,0:T(8,128)}, f32[30,240]{1,0:T(8,128)}, /*index=5*/f32[1,15]{1,0:T(1,128)}) custom-call(bf16[960,256]{1,0:T(8,128)(2,1)} %get-tuple-element.18.refs_0_, bf16[960,256]{1,0:T(8,128)(2,1)} %get-tuple-element.19.refs_1_, ...), custom_call_target="tpu_custom_call" | custom-call | bytes 3000000 | tf_op jit(solution)/shard_map/pallas_call | solution.py:806
Async XLA Ops:
  0.6 0.7 copy-start

commit v6 on v5

--- a/solution.py
+++ b/solution.py
@@ -254,9 +254,37 @@
         if h == 1:
             await_bytes(kt.at[yo], ks_v)
             to_chips(kt, ka_s, ka_v)
-        else:
-            to_mate(kt, ka_v, kb_s, kb_v)
         send_part(1, *first)
+
+    for copy in rest_here:
+        copy.wait()
+    for g in range(GROUPS):
+        xg[g] = dot_nt(eye[...], xv[g]).astype(BF)
+        cotv[g, pl.ds(DG, PIECE)] = jnp.zeros((PIECE, 256), BF)
+    mint[...] = dot_nt(eye[...], min_ref[...]).astype(BF)
+    moutt[...] = dot_nt(eye[...], mout_ref[...]).astype(BF)
+    row, lane = iotas((256, 256))
+    chosen = ones_where((lane == 4 * (row & 63) + (row >> 6)) & ((row & 63) < 60))
+    placed = ones_where((row == 60 * (lane >> 6) + (lane & 63)) & ((lane & 63) < 60))
+    chosen_rows = [dot(chosen, cotv[part]).astype(BF) for part in range(GROUPS)]
+    gain_rows = jnp.broadcast_to(gain_ref[...].astype(F32).reshape(1, D), (PIECE, D)).astype(BF)
+    for g in range(GROUPS):
+        cotn[g] = dot_nt(eye[...], cotv[g]).astype(BF)
+        lined = jnp.concatenate([chosen_rows[part][64 * g : 64 * g + 64] for part in range(GROUPS)], axis=0)
+        cotg[g] = dot_nt(eye[...], dot(placed, lined).astype(BF)).astype(BF)
+        low, high = GAIN_WINDOWS[g]
+        channel, lane = iotas((high - low, 256))
+        gaing[g] = dot(gain_rows[:, low:high], ones_where((channel + low == g * DG + lane) & (lane < DG)))[0:8]
+    to_mate(kt, ka_v, kb_s, kb_v)
+    for g in range(GROUPS):
+        low, high = HIDDEN_WINDOWS[g]
+        column, hidden_unit = iotas((high - low, 512))
+        chosen = (column + low == g * FFG + hidden_unit - 2 * (hidden_unit >> 5)) & ((hidden_unit & 31) < 30)
+        chooser = ones_where(chosen)
+        upp[g, 0:DG] = dot(up_ref[:, low:high], chooser).astype(BF)
+        dnp[g, 0:DG] = dot(down_ref[:, low:high], chooser).astype(BF)
+        upp[g, DG:256] = jnp.zeros((256 - DG, 512), BF)
+        dnp[g, DG:256] = jnp.zeros((256 - DG, 512), BF)
 
     def spread_twiddles(which, p, q, slab):
         wide = slab.astype(F32)
@@ -338,36 +366,6 @@
         two_at_once(column_of, load_wide, 1, high_bits, False, leave)
         for part in range(2):
             send_part(part, *half_of(h, src2, m2, s2, v2, (z, y), z))
-        if h == 1:
-            for copy in rest_here:
-                copy.wait()
-            for g in range(GROUPS):
-                xg[g] = dot_nt(eye[...], xv[g]).astype(BF)
-                cotv[g, pl.ds(DG, PIECE)] = jnp.zeros((PIECE, 256), BF)
-            mint[...] = dot_nt(eye[...], min_ref[...]).astype(BF)
-            moutt[...] = dot_nt(eye[...], mout_ref[...]).astype(BF)
-            for g in range(GROUPS):
-                cotn[g] = dot_nt(eye[...], cotv[g]).astype(BF)
-                picked = jnp.zeros((256, 256), F32)
-                for part in range(GROUPS):
-                    j, lane = iotas((256, 256))
-                    picked = picked + dot(ones_where((part * DG + lane == 4 * j + g) & (lane < DG)), cotv[part])
-                cotg[g] = dot_nt(eye[...], picked.astype(BF)).astype(BF)
-                low, high = GAIN_WINDOWS[g]
-                channel, lane = iotas((high - low, 256))
-                gain_rows = jnp.broadcast_to(gain_ref[:, low:high].astype(F32), (PIECE, high - low)).astype(BF)
-                gaing[g] = dot(gain_rows, ones_where((channel + low == g * DG + lane) & (lane < DG)))[0:8]
-
-
-    for g in range(GROUPS):
-        low, high = HIDDEN_WINDOWS[g]
-        column, hidden_unit = iotas((high - low, 512))
-        chosen = (column + low == g * FFG + hidden_unit - 2 * (hidden_unit >> 5)) & ((hidden_unit & 31) < 30)
-        chooser = ones_where(chosen)
-        upp[g, 0:DG] = dot(up_ref[:, low:high], chooser).astype(BF)
-        dnp[g, 0:DG] = dot(down_ref[:, low:high], chooser).astype(BF)
-        upp[g, DG:256] = jnp.zeros((256 - DG, 512), BF)
-        dnp[g, DG:256] = jnp.zeros((256 - DG, 512), BF)
 
     for g in range(GROUPS):
         acot[g] = dot(cotg[g], dnp[g])
@@ -416,22 +414,6 @@
         means = means + jnp.sum(ngr[g] * gaing[g, 0:1] * hg[g].astype(F32), axis=1, keepdims=True)
     scale_column = rowscale[:, 0:1]
     means = means * (1.0 / D) * scale_column * scale_column * scale_column
-    def split_terms(kind, g, term):
-        split = term.astype(BF).reshape(16, 2, PIECE, 256)
-        for half in range(2):
-            for side in range(2):
-                gg[side, 2 * kind + half, pl.ds(g * 16, 16)] = split[:, half, :, side * 128 : side * 128 + 128]
-
-    def weight_terms():
-        row_here = (lax.broadcasted_iota(jnp.int32, (512, 256), 0) & 31) == 30
-        for g in range(GROUPS):
-            split_terms(1, g, dot_tn(act[:, pl.ds(g * 512, 512)], cotg[g]))
-        send(gg.at[1 - core, pl.ds(2, 2)], r1a.at[pl.ds(2, 2)], ga_s.at[1], ga_v.at[1], (mate, me))
-        for g in range(GROUPS):
-            gain_term = jnp.sum(ngr[g] * hg[g].astype(F32) * rowscale[:, 0:1], axis=0, keepdims=True)
-            split_terms(0, g, jnp.where(row_here, gain_term, dot_tn(pgr[g], ng[g])))
-        send(gg.at[1 - core, pl.ds(0, 2)], r1a.at[pl.ds(0, 2)], ga_s.at[0], ga_v.at[0], (mate, me))
-
     for h in (1, 0):
         lanes = slice(128 * h, 128 * h + 128)
         for pair in range(2):
@@ -442,11 +424,21 @@
             store_half(src3, h, pair, dot(moutt[...], half_lanes(hgr, h, pair)).astype(BF))
         for part in range(2):
             send_part(part, *half_of(h, src3, a3, s3, v3, (y, z), y))
-        if h == 1:
-            weight_terms()
-
-    for kind in (1, 0):
-        await_bytes(r1a.at[pl.ds(2 * kind, 2)], ga_v.at[kind])
+
+    row_here = (lax.broadcasted_iota(jnp.int32, (512, 256), 0) & 31) == 30
+    for g in range(GROUPS):
+        gain_term = jnp.sum(ngr[g] * hg[g].astype(F32) * rowscale[:, 0:1], axis=0, keepdims=True)
+        up_term = jnp.where(row_here, gain_term, dot_tn(pgr[g], ng[g]))
+        down_term = dot_tn(act[:, pl.ds(g * 512, 512)], cotg[g])
+        for kind, term in ((0, up_term), (1, down_term)):
+            split = term.astype(BF).reshape(16, 2, PIECE, 256)
+            for half in range(2):
+                for side in range(2):
+                    gg[side, 2 * kind + half, pl.ds(g * 16, 16)] = split[:, half, :, side * 128 : side * 128 + 128]
+
+    send(gg.at[1 - core], r1a, ga_s, ga_v, (mate, me))
+
+    await_bytes(r1a, ga_v)
 
     def pair_sum(step):
         for slab in range(4):
@@ -702,8 +694,7 @@
 
     await_bytes(kt.at[0], ka_s.at[0])
     await_bytes(kgf.at[0], kh_s.at[0])
-    for kind in range(2):
-        await_bytes(r1a.at[pl.ds(0, 2)], ga_s.at[kind])
+    await_bytes(r1a, ga_s)
     await_bytes(kra, kr_s)
 
     def chips_left(step):
@@ -757,7 +748,7 @@
     wide = (D, 256)
     scratch = dict(
         xv=grouped, kv=grouped, cotv=grouped, min_ref=square, mout_ref=square,
-        ts_ref=vmem((6, 2, 256), BF), tc_ref=vmem((6, 2, 256), BF), gain_ref=vmem((1, D), BF),
+        ts_ref=vmem((6, 2, 256), BF), tc_ref=vmem((6, 2, 256), BF), gain_ref=vmem((D,), BF),
         up_ref=vmem((DG, 1920), BF), down_ref=vmem((DG, 1920), BF),
         outv=vmem(wide, BF), igv=vmem(wide, BF), kgv=vmem(wide, BF),
         ugv=vmem((30, DG), F32), dgv=vmem((30, DG), F32), gnv=vmem((1, 15), F32),
@@ -784,7 +775,7 @@
         ks_s=dma((2,)), ks_v=dma, ka_s=dma((4,)), ka_v=dma((4,)), kb_s=dma((4,)), kb_v=dma((4,)),
         kr_s=dma, kr_v=dma, kc_s=dma((4,)), kc_v=dma((4,)), kf_s=dma((2,)), kf_v=dma,
         kh_s=dma((4,)), kh_v=dma((4,)), ki_s=dma((4,)), ki_v=dma((4,)),
-        ga_s=dma((2,)), ga_v=dma((2,)), gb_s=dma((4,)), gb_v=dma((4,)), gf_s=dma((SIDE,)), gf_v=dma((SIDE,)),
+        ga_s=dma, ga_v=dma, gb_s=dma((4,)), gb_v=dma((4,)), gf_s=dma((SIDE,)), gf_v=dma((SIDE,)),
     )
     shape = jax.ShapeDtypeStruct
     results = [shape(wide, BF)] * 3 + [shape((30, DG), F32)] * 2 + [shape((1, 15), F32)]
@@ -801,7 +792,7 @@
     )(
         inputs[0].T, cotangent[0].T, kernel_values.T, mix_in, mix_out,
         twiddle_self.transpose(1, 0, 2), twiddle_cross.transpose(1, 0, 2),
-        norm_gain[None, :], up_weight, down_weight,
+        norm_gain, up_weight, down_weight,
     )
     output, input_grad, kernel_grad, up_grad, down_grad, gain_grad = pl.pallas_call(
         settle,

time: 109 us -> 108 us (level)
  local copies, waits for them, and re-layouts: 1.27 us -> 0 us
where the time goes in v6:
time: 108 us; the launch traced here: 107 us
  Pallas kernels  107 us (99%)
    pallas_call x1, Pallas kernels, local(): pl.pallas_call(kernel, out_shape=results, in_specs=[hbm] * 10, out_specs=...  104 us
    pallas_call x1, Pallas kernels, local(): pl.pallas_call(settle, out_shape=results, in_specs=[hbm] * 6, out_specs=[...  2.25 us

profile of v6, /device:TPU:1, one launch (start us, length us, event | category | flops | bytes accessed | tf_op | source)
XLA Modules:
  0.0 107.4 jit_solution(12204489469710219673)
XLA Ops:
  0.6 104.3 %shard_map.145 = (bf16[960,256]{1,0:T(8,128)(2,1)}, bf16[960,256]{1,0:T(8,128)(2,1)}, bf16[960,256]{1,0:T(8,128)(2,1)}, f32[30,240]{1,0:T(8,128)}, f32[30,240]{1,0:T(8,128)}, /*index=5*/f32[1,15]{1,0:T(1,128)}) custom-call(bf16[960,256]{1,0:T(8,128)(2,1)} %bitcast.19, bf16[960,256]{1,0:T(8,128)(2,1)} %bitcast.20, bf16[960,256]{1,0:T(8,128)(2,1)} %bitcast.21, ...), custom_call_target="tpu_custom_call" | custom-call | flops 4000000000 | bytes 6000000 | tf_op jit(solution)/shard_map/pallas_call | solution.py:782
  105.0 2.2 %shard_map.146 = (bf16[960,256]{1,0:T(8,128)(2,1)}, bf16[960,256]{1,0:T(8,128)(2,1)}, bf16[960,256]{1,0:T(8,128)(2,1)}, f32[30,240]{1,0:T(8,128)}, f32[30,240]{1,0:T(8,128)}, /*index=5*/f32[1,15]{1,0:T(1,128)}) custom-call(bf16[960,256]{1,0:T(8,128)(2,1)} %get-tuple-element.18.refs_0_, bf16[960,256]{1,0:T(8,128)(2,1)} %get-tuple-element.19.refs_1_, ...), custom_call_target="tpu_custom_call" | custom-call | bytes 3000000 | tf_op jit(solution)/shard_map/pallas_call | solution.py:797

commit v7 on v3

--- a/solution.py
+++ b/solution.py
@@ -260,17 +260,18 @@
         cotv[g, pl.ds(DG, PIECE)] = jnp.zeros((PIECE, 256), BF)
     mint[...] = dot_nt(eye[...], min_ref[...]).astype(BF)
     moutt[...] = dot_nt(eye[...], mout_ref[...]).astype(BF)
+    row, lane = iotas((256, 256))
+    chosen = ones_where((lane == 4 * (row & 63) + (row >> 6)) & ((row & 63) < 60))
+    placed = ones_where((row == 60 * (lane >> 6) + (lane & 63)) & ((lane & 63) < 60))
+    chosen_rows = [dot(chosen, cotv[part]).astype(BF) for part in range(GROUPS)]
+    gain_rows = jnp.broadcast_to(gain_ref[...].astype(F32).reshape(1, D), (PIECE, D)).astype(BF)
     for g in range(GROUPS):
         cotn[g] = dot_nt(eye[...], cotv[g]).astype(BF)
-        picked = jnp.zeros((256, 256), F32)
-        for part in range(GROUPS):
-            j, lane = iotas((256, 256))
-            picked = picked + dot(ones_where((part * DG + lane == 4 * j + g) & (lane < DG)), cotv[part])
-        cotg[g] = dot_nt(eye[...], picked.astype(BF)).astype(BF)
+        lined = jnp.concatenate([chosen_rows[part][64 * g : 64 * g + 64] for part in range(GROUPS)], axis=0)
+        cotg[g] = dot_nt(eye[...], dot(placed, lined).astype(BF)).astype(BF)
         low, high = GAIN_WINDOWS[g]
         channel, lane = iotas((high - low, 256))
-        gain_rows = jnp.broadcast_to(gain_ref[:, low:high].astype(F32), (PIECE, high - low)).astype(BF)
-        gaing[g] = dot(gain_rows, ones_where((channel + low == g * DG + lane) & (lane < DG)))[0:8]
+        gaing[g] = dot(gain_rows[:, low:high], ones_where((channel + low == g * DG + lane) & (lane < DG)))[0:8]
     to_mate(kt, ka_v, kb_s, kb_v)
     for g in range(GROUPS):
         low, high = HIDDEN_WINDOWS[g]
@@ -744,7 +745,7 @@
     wide = (D, 256)
     scratch = dict(
         xv=grouped, kv=grouped, cotv=grouped, min_ref=square, mout_ref=square,
-        ts_ref=vmem((6, 2, 256), BF), tc_ref=vmem((6, 2, 256), BF), gain_ref=vmem((1, D), BF),
+        ts_ref=vmem((6, 2, 256), BF), tc_ref=vmem((6, 2, 256), BF), gain_ref=vmem((D,), BF),
         up_ref=vmem((DG, 1920), BF), down_ref=vmem((DG, 1920), BF),
         outv=vmem(wide, BF), igv=vmem(wide, BF), kgv=vmem(wide, BF),
         ugv=vmem((30, DG), F32), dgv=vmem((30, DG), F32), gnv=vmem((1, 15), F32),
@@ -788,7 +789,7 @@
     )(
         inputs[0].T, cotangent[0].T, kernel_values.T, mix_in, mix_out,
         twiddle_self.transpose(1, 0, 2), twiddle_cross.transpose(1, 0, 2),
-        norm_gain[None, :], up_weight, down_weight,
+        norm_gain, up_weight, down_weight,
     )
     output, input_grad, kernel_grad, up_grad, down_grad, gain_grad = pl.pallas_call(
         settle,

time: 104 us -> 103 us (level)
  local copies, waits for them, and re-layouts: 1.27 us -> 0 us
where the time goes in v7:
time: 103 us
  Pallas kernels  102 us (99%)
    pallas_call x1, Pallas kernels, local(): pl.pallas_call(kernel, out_shape=results, in_specs=[hbm] * 10, out_specs=...  99.5 us
    pallas_call x1, Pallas kernels, local(): pl.pallas_call(settle, out_shape=results, in_specs=[hbm] * 6, out_specs=[...  2.25 us

profile of v7, /device:TPU:1, one launch (start us, length us, event | category | flops | bytes accessed | tf_op | source)
XLA Modules:
  0.0 102.5 jit_solution(5789487417247764442)
XLA Ops:
  0.6 99.5 %shard_map.145 = (bf16[960,256]{1,0:T(8,128)(2,1)}, bf16[960,256]{1,0:T(8,128)(2,1)}, bf16[960,256]{1,0:T(8,128)(2,1)}, f32[30,240]{1,0:T(8,128)}, f32[30,240]{1,0:T(8,128)}, /*index=5*/f32[1,15]{1,0:T(1,128)}) custom-call(bf16[960,256]{1,0:T(8,128)(2,1)} %bitcast.19, bf16[960,256]{1,0:T(8,128)(2,1)} %bitcast.20, bf16[960,256]{1,0:T(8,128)(2,1)} %bitcast.21, ...), custom_call_target="tpu_custom_call" | custom-call | flops 4000000000 | bytes 6000000 | tf_op jit(solution)/shard_map/pallas_call | solution.py:779
  100.1 2.2 %shard_map.146 = (bf16[960,256]{1,0:T(8,128)(2,1)}, bf16[960,256]{1,0:T(8,128)(2,1)}, bf16[960,256]{1,0:T(8,128)(2,1)}, f32[30,240]{1,0:T(8,128)}, f32[30,240]{1,0:T(8,128)}, /*index=5*/f32[1,15]{1,0:T(1,128)}) custom-call(bf16[960,256]{1,0:T(8,128)(2,1)} %get-tuple-element.18.refs_0_, bf16[960,256]{1,0:T(8,128)(2,1)} %get-tuple-element.19.refs_1_, ...), custom_call_target="tpu_custom_call" | custom-call | bytes 3000000 | tf_op jit(solution)/shard_map/pallas_call | solution.py:794
